TPU v7x, 256 devices: a whole 4x4x8 slice. The times are simulated.
256 devices in a mesh: pb: 2 (over core), pas: 16 (over x, z_lo), tp: 8 (over z_hi, y).
Axes of the slice: x: 4, y: 4, z: 8 (z_hi: 2, z_lo: 4; z = z_hi * 4 + z_lo), core: 2. Of those that a mesh axis runs over, the one named last changes fastest.
Arguments:
- token_ids: int32 [8], P('pb'), parts along dimension 0, may hold values from 0 to 32127
- embedding: bfloat16 [32128, 4096], P(('pas', 'tp')), may hold values from -6 to 6
- passages: bfloat16 [16384, 4096], P(('pb', 'pas'), 'tp'), parts along dimension 0, may hold values from -6 to 6
- passage_lengths: int32 [64], P(('pb', 'pas')), parts along dimension 0, may hold values from 32 to 256
- w_key: bfloat16 [4096, 4096], P('pas', 'tp'), may hold values from -0.09375 to 0.09375
- w_value: bfloat16 [4096, 4096], P('pas', 'tp'), may hold values from -0.09375 to 0.09375
- norm_self: float32 [4096], replicated, may hold values from 0.1 to 1.9
- w_self_query: bfloat16 [4096, 4096], P('pas', 'tp'), may hold values from -1 to 1
- w_self_key: bfloat16 [4096, 4096], P('pas', 'tp'), may hold values from -0.09375 to 0.09375
- w_self_value: bfloat16 [4096, 4096], P('pas', 'tp'), may hold values from -0.09375 to 0.09375
- w_self_out: bfloat16 [4096, 4096], P('tp', 'pas'), may hold values from -0.09375 to 0.09375
- norm_cross: float32 [4096], replicated, may hold values from 0.1 to 1.9
- w_cross_query: bfloat16 [4096, 4096], P('pas', 'tp'), may hold values from -1 to 1
- w_cross_out: bfloat16 [4096, 4096], P('tp', 'pas'), may hold values from -0.09375 to 0.09375
- norm_ffn: float32 [4096], replicated, may hold values from 0.1 to 1.9
- w_gate: bfloat16 [4096, 10240], P('pas', 'tp'), may hold values from -0.09375 to 0.09375
- w_up: bfloat16 [4096, 10240], P('pas', 'tp'), may hold values from -0.09375 to 0.09375
- w_down: bfloat16 [10240, 4096], P('tp', 'pas'), may hold values from -0.0625 to 0.0625
Outputs:
- layer_out: float32 [8, 4096], P('pb', ('pas', 'tp')), parts along dimension 0
- cross_keys: bfloat16 [16384, 4096], P(('pb', 'pas'), 'tp'), parts along dimension 0
- cross_values: bfloat16 [16384, 4096], P(('pb', 'pas'), 'tp'), parts along dimension 0
There are 2 independent parts, one for each index of `pb`. A program takes and returns all parts, laid end to end along the dimension named above; an argument that names none is the same for every part. Nothing has to cross between parts.
All inputs are finite; a program needn't handle non-finite values.
Results may differ from a plain program's by a relative error of at most 0.025.
Values may be sent and summed in bfloat16 or wider, within the bound.
A program may use at most 128 MiB of HBM per device.

v0:
```python
import jax
import jax.numpy as jnp
from jax import lax
from jax.sharding import PartitionSpec as P

D = 4096
DH = 64
PLEN = 256


def rms_norm(state, gain):
    mean_sq = jnp.mean(state * state, axis=-1, keepdims=True)
    return (state * lax.rsqrt(mean_sq + 1e-06) * gain).astype(jnp.bfloat16)


def width_part(normed, weight):
    rows = weight.shape[0]
    start = lax.axis_index("pas") * rows
    own = lax.dynamic_slice_in_dim(normed, start, rows, 1)
    return jnp.dot(own, weight, preferred_element_type=jnp.float32)


def project_out(inner, weight):
    term = jnp.dot(inner, weight, preferred_element_type=jnp.float32)
    summed = lax.psum(term, "tp")
    return lax.all_gather(summed, "pas", axis=1, tiled=True)


def cross_step(query, carry, pieces):
    keys_blk, values_blk, lengths_blk = pieces
    peak, total, accum = carry
    count = keys_blk.shape[0]
    heads = query.shape[0]
    keys_h = keys_blk.reshape(count, heads, DH)
    values_h = values_blk.reshape(count, heads, DH)
    scores = jnp.einsum("hsd,nhd->hsn", query, keys_h, preferred_element_type=jnp.float32) * (
        1.0 / DH**0.5
    )
    live = (jnp.arange(PLEN)[None, :] < lengths_blk[:, None]).reshape(count)
    scores = jnp.where(live[None, None], scores, -1e30)
    new_peak = jnp.maximum(peak, jnp.max(scores, axis=-1))
    weights = jnp.where(live[None, None], jnp.exp(scores - new_peak[..., None]), 0.0).astype(
        jnp.bfloat16
    )
    total = jnp.sum(weights.astype(jnp.float32), axis=-1)
    accum = jnp.einsum("hsn,nhd->hsd", weights, values_h, preferred_element_type=jnp.float32)
    return (new_peak, total, accum)


def shards(
    token_ids,
    embedding,
    passages,
    passage_lengths,
    w_key,
    w_value,
    norm_self,
    w_self_query,
    w_self_key,
    w_self_value,
    w_self_out,
    norm_cross,
    w_cross_query,
    w_cross_out,
    norm_ffn,
    w_gate,
    w_up,
    w_down,
):
    scale = 1.0 / DH**0.5
    steps = token_ids.shape[0]
    whole_rows = lax.all_gather(passages, "tp", axis=1, tiled=True)
    width_cols = w_key.shape[1]
    key_sum = jnp.dot(
        whole_rows,
        lax.all_gather(w_key, "pas", axis=0, tiled=True),
        preferred_element_type=jnp.float32,
    )
    value_sum = jnp.dot(
        whole_rows,
        lax.all_gather(w_value, "pas", axis=0, tiled=True),
        preferred_element_type=jnp.float32,
    )
    cross_keys = key_sum.astype(jnp.bfloat16)
    cross_values = value_sum.astype(jnp.bfloat16)
    vocab_rows = embedding.shape[0]
    offset = lax.axis_index(("pas", "tp")) * vocab_rows
    onehot = (
        token_ids[:, None] == offset + jnp.arange(vocab_rows, dtype=jnp.int32)[None, :]
    ).astype(jnp.bfloat16)
    state = lax.psum(jnp.dot(onehot, embedding, preferred_element_type=jnp.float32), ("pas", "tp"))
    heads = width_cols // DH
    normed = rms_norm(state, norm_self)
    query_sum, key_part, value_part = lax.psum(
        (
            width_part(normed, w_self_query),
            width_part(normed, w_self_key),
            width_part(normed, w_self_value),
        ),
        "pas",
    )
    query = query_sum.astype(jnp.bfloat16).reshape(steps, heads, DH)
    keyed = key_part.astype(jnp.bfloat16).reshape(steps, heads, DH)
    valued = value_part.astype(jnp.bfloat16).reshape(steps, heads, DH)
    scores = jnp.einsum("shd,rhd->hsr", query, keyed, preferred_element_type=jnp.float32) * scale
    causal = jnp.arange(steps)[:, None] >= jnp.arange(steps)[None, :]
    scores = jnp.where(causal[None], scores, -1e30)
    peak = jnp.max(scores, axis=-1, keepdims=True)
    weights = jnp.where(causal[None], jnp.exp(scores - peak), 0.0).astype(jnp.bfloat16)
    total = jnp.sum(weights.astype(jnp.float32), axis=-1)
    mixed = (
        jnp.einsum("hsr,rhd->hsd", weights, valued, preferred_element_type=jnp.float32)
        / total[..., None]
    )
    self_heads = jnp.transpose(mixed, (1, 0, 2)).astype(jnp.bfloat16).reshape(steps, heads * DH)
    state = state + project_out(self_heads, w_self_out)
    normed = rms_norm(state, norm_cross)
    cquery = lax.psum(width_part(normed, w_cross_query), "pas")
    cquery = jnp.transpose(cquery.astype(jnp.bfloat16).reshape(steps, heads, DH), (1, 0, 2))
    start_carry = (
        jnp.full((heads, steps), -1e30, jnp.float32),
        jnp.zeros((heads, steps), jnp.float32),
        jnp.zeros((heads, steps, DH), jnp.float32),
    )
    peak_all, total_all, accum_all = cross_step(
        cquery,
        start_carry,
        (
            lax.all_gather(cross_keys, "pas", axis=0, tiled=True),
            lax.all_gather(cross_values, "pas", axis=0, tiled=True),
            lax.all_gather(passage_lengths, "pas", axis=0, tiled=True),
        ),
    )
    cmixed = accum_all / total_all[..., None]
    cross_heads = jnp.transpose(cmixed, (1, 0, 2)).astype(jnp.bfloat16).reshape(steps, heads * DH)
    state = state + project_out(cross_heads, w_cross_out)
    normed = rms_norm(state, norm_ffn)
    gated, upper = lax.psum((width_part(normed, w_gate), width_part(normed, w_up)), "pas")
    hidden = (jax.nn.gelu(gated, approximate=True) * upper).astype(jnp.bfloat16)
    state = state + project_out(hidden, w_down)
    out_cols = D // (lax.axis_size("pas") * lax.axis_size("tp"))
    layer_out = lax.dynamic_slice_in_dim(
        state, lax.axis_index(("pas", "tp")) * out_cols, out_cols, 1
    )
    return (layer_out, cross_keys, cross_values)


def solution(mesh):
    in_specs = (
        P("pb"),
        P(("pas", "tp"), None),
        P(("pb", "pas"), "tp"),
        P(("pb", "pas")),
        P("pas", "tp"),
        P("pas", "tp"),
        P(),
        P("pas", "tp"),
        P("pas", "tp"),
        P("pas", "tp"),
        P("tp", "pas"),
        P(),
        P("pas", "tp"),
        P("tp", "pas"),
        P(),
        P("pas", "tp"),
        P("pas", "tp"),
        P("tp", "pas"),
    )
    out_specs = (P("pb", ("pas", "tp")), P(("pb", "pas"), "tp"), P(("pb", "pas"), "tp"))
    return jax.shard_map(shards, mesh=mesh, in_specs=in_specs, out_specs=out_specs, check_vma=False)
```

profile of v0, /device:TPU:6, one launch (start us, length us, event | category | flops | bytes accessed | tf_op | source)
XLA Modules:
  0.0 937.7 jit_solution(16281023076063458184)
XLA Ops:
  8.0 0.0 copy-start
  8.0 0.0 all-gather.6.cloned.1.call-start
  8.1 0.7 all-gather.6.cloned.1.call-update
  8.7 0.0 all-gather.8.cloned.1.call-start
  8.8 0.7 all-gather.8.cloned.1.call-update
  9.5 0.0 all-gather.12.cloned.1.call-start
  9.5 0.7 all-gather.12.cloned.1.call-update
  10.2 0.0 all-reduce.5.cloned.1.call-start
  10.3 1.7 fusion.37
  12.0 0.0 all-reduce.5.cloned.1.call-update
  12.0 0.0 all-gather.10.cloned.1.call-start
  12.1 113.9 %all-gather.6.cloned.1.call-done = bf16[512,4096]{1,0:T(8,128)(2,1)} async-done(((bf16[512,512]{1,0:T(8,128)(2,1)}), bf16[512,4096]{1,0:T(8,128)(2,1)}) %all-gather.6.cloned.1.call-update) | async-done | bytes 4194320 | tf_op jit(solution)/shard_map/all_gather | solution.py:72
  126.0 99.0 %all-gather.8.cloned.1.call-done = bf16[4096,512]{1,0:T(8,128)(2,1)} async-done(((bf16[256,512]{1,0:T(8,128)(2,1)}), bf16[4096,512]{1,0:T(8,128)(2,1)}) %all-gather.8.cloned.1.call-update) | async-done | bytes 4194320 | tf_op jit(solution)/shard_map/all_gather | solution.py:76
  225.0 6.6 convolution_convert_fusion.1
  231.6 0.0 all-gather.10.cloned.1.call-update
  231.6 0.0 copy-start.7
  231.6 0.0 copy-start.6
  231.7 0.0 all-gather.14.cloned.1.call-start
  231.7 95.0 %all-gather.12.cloned.1.call-done = bf16[4096,512]{1,0:T(8,128)(2,1)} async-done(((bf16[256,512]{1,0:T(8,128)(2,1)}), bf16[4096,512]{1,0:T(8,128)(2,1)}) %all-gather.12.cloned.1.call-update) | async-done | bytes 4194320 | tf_op jit(solution)/shard_map/all_gather | solution.py:81
  326.8 6.6 convolution_convert_fusion
  333.3 0.0 all-gather.14.cloned.1.call-update
  333.4 0.8 dynamic-slice.1
  334.1 0.8 dynamic-slice.2
  334.9 0.6 dynamic-slice
  336.2 0.2 dynamic-update-slice
  336.4 12.3 %all-reduce = s32[32]{0:T(128)S(1)} all-reduce(s32[32]{0:T(128)S(1)} %dynamic-update-slice), channel_id=1, replica_groups=mesh['pb'=2,'pas'=16,'tp'=8] {'pas'}, use_global_device_ids=true, to_apply=%add | all-reduce | flops 32 | bytes 256
  348.7 0.1 iota_compare_fusion
  348.8 0.8 dynamic-slice.3
  349.6 1.0 multiply_reduce_fusion.2
  350.6 0.9 fusion.67
  351.5 0.9 fusion.65
  352.3 0.9 fusion.63
  353.2 74.1 %all-reduce.2 = (bf16[4,512]{1,0:T(4,128)(2,1)S(1)}, bf16[4,512]{1,0:T(4,128)(2,1)S(1)}, bf16[4,512]{1,0:T(4,128)(2,1)S(1)}) all-reduce(f32[4,512]{1,0:T(4,128)S(1)} %fusion.63, f32[4,512]{1,0:T(4,128)S(1)} %fusion.65, f32[4,512]{1,0:T(4,128)S(1)} %fusion.67), channel_id=1, replica_groups=mesh['pb'=2,'pas'=16,'tp'=8] {'pas'}, use_global_device_ids=true, to_apply=%region_3.0 | all-reduce | flops 6144 | bytes 36864 | tf_op jit(solution)/shard_map/psum | solution.py:94
  427.2 0.1 reshape.96
  427.3 0.1 reshape.97
  427.4 0.1 reshape.98
  427.5 0.2 convert_reduce_fusion.1
  427.6 0.2 fusion.8
  427.8 0.1 reshape.99
  427.9 0.1 fusion.69
  428.1 29.7 %psum.74 = f32[4,256]{1,0:T(4,128)S(1)} all-reduce(f32[4,256]{1,0:T(4,128)S(1)} %fusion.69), channel_id=1, replica_groups=mesh['pb'=2,'pas'=16,'tp'=8] {'tp'}, use_global_device_ids=true, to_apply=%region_7.8 | all-reduce | flops 1024 | bytes 8192 | tf_op jit(solution)/shard_map/psum | solution.py:25
  457.8 40.5 %all_gather.27 = f32[4,4096]{1,0:T(4,128)S(1)} all-gather(f32[4,256]{1,0:T(4,128)S(1)} %psum.74), channel_id=1, replica_groups=mesh['pb'=2,'pas'=16,'tp'=8] {'pas'}, dimensions={1}, use_global_device_ids=true | all-gather | bytes 69632 | tf_op jit(solution)/shard_map/all_gather | solution.py:26
  498.3 1.0 multiply_reduce_fusion.1
  499.4 1.1 fusion.39
  500.5 39.1 %psum.75 = bf16[4,512]{1,0:T(4,128)(2,1)S(1)} all-reduce(f32[4,512]{1,0:T(4,128)S(1)} %fusion.39), channel_id=1, replica_groups=mesh['pb'=2,'pas'=16,'tp'=8] {'pas'}, use_global_device_ids=true, to_apply=%region_9.10 | all-reduce | flops 2048 | bytes 12288 | tf_op jit(solution)/shard_map/psum | solution.py:118
  539.6 0.1 reshape.100
  539.7 11.3 %copy.34 = bf16[8192,512]{0,1:T(8,128)(2,1)} copy(bf16[8192,512]{1,0:T(8,128)(2,1)} %all-gather.10.cloned.1.call-done) | data formatting | bytes 16777216 | tf_op jit(solution)/shard_map/all_gather | solution.py:129
  551.0 4.7 fusion.62
  555.8 0.6 convert_reduce_fusion
  556.4 151.5 %all-gather.14.cloned.1.call-done = bf16[8192,512]{1,0:T(8,128)(2,1)} async-done(((bf16[512,512]{1,0:T(8,128)(2,1)}), bf16[8192,512]{1,0:T(8,128)(2,1)}) %all-gather.14.cloned.1.call-update) | async-done | bytes 8388624 | tf_op jit(solution)/shard_map/all_gather | solution.py:130
  707.9 11.4 %copy.35 = bf16[8192,512]{0,1:T(8,128)(2,1)} copy(bf16[8192,512]{1,0:T(8,128)(2,1)} %all-gather.14.cloned.1.call-done) | data formatting | bytes 16777216 | tf_op jit(solution)/shard_map/all_gather | solution.py:130
  719.3 5.7 fusion.9
  725.1 0.1 reshape.103
  725.2 0.2 fusion.70
  725.3 28.9 %psum.76 = f32[4,256]{1,0:T(4,128)S(1)} all-reduce(f32[4,256]{1,0:T(4,128)S(1)} %fusion.70), channel_id=1, replica_groups=mesh['pb'=2,'pas'=16,'tp'=8] {'tp'}, use_global_device_ids=true, to_apply=%region_12.13 | all-reduce | flops 1024 | bytes 8192 | tf_op jit(solution)/shard_map/psum | solution.py:25
  754.2 35.0 %all_gather.34 = f32[4,4096]{1,0:T(4,128)S(1)} all-gather(f32[4,256]{1,0:T(4,128)S(1)} %psum.76), channel_id=1, replica_groups=mesh['pb'=2,'pas'=16,'tp'=8] {'pas'}, dimensions={1}, use_global_device_ids=true | all-gather | bytes 69632 | tf_op jit(solution)/shard_map/all_gather | solution.py:26
  789.3 0.1 multiply_reduce_fusion
  789.4 1.3 fusion.54
  790.7 1.3 fusion.56
  792.1 74.7 %all-reduce.1 = (f32[4,1280]{1,0:T(4,128)S(1)}, f32[4,1280]{1,0:T(4,128)S(1)}) all-reduce(f32[4,1280]{1,0:T(4,128)S(1)} %fusion.56, f32[4,1280]{1,0:T(4,128)S(1)} %fusion.54), channel_id=1, replica_groups=mesh['pb'=2,'pas'=16,'tp'=8] {'pas'}, use_global_device_ids=true, to_apply=%region_15.16 | all-reduce | flops 10240 | bytes 81920 | tf_op jit(solution)/shard_map/psum | solution.py:138
  866.8 1.3 fusion.20
  868.0 23.8 %psum.79 = f32[4,256]{1,0:T(4,128)S(1)} all-reduce(f32[4,256]{1,0:T(4,128)S(1)} %fusion.20), channel_id=1, replica_groups=mesh['pb'=2,'pas'=16,'tp'=8] {'tp'}, use_global_device_ids=true, to_apply=%region_16.17 | all-reduce | flops 1024 | bytes 8192 | tf_op jit(solution)/shard_map/psum | solution.py:25
  891.8 38.1 %all_gather.35 = f32[4,4096]{1,0:T(4,128)S(1)} all-gather(f32[4,256]{1,0:T(4,128)S(1)} %psum.79), channel_id=1, replica_groups=mesh['pb'=2,'pas'=16,'tp'=8] {'pas'}, dimensions={1}, use_global_device_ids=true | all-gather | bytes 69632 | tf_op jit(solution)/shard_map/all_gather | solution.py:26
  930.0 0.7 dynamic-slice_add_fusion
  (25 shorter events, 0.1 us)
Async XLA Ops:
  8.0 2.3 copy-start
  8.0 118.0 %all-gather.6.cloned.1.call-start = ((), (), s32[]{:S(2)}) async-start(), calls=%async_computation.1 | async-start | bytes 4718592 | tf_op jit(solution)/shard_map/all_gather | solution.py:72
  8.7 216.2 %all-gather.8.cloned.1.call-start = ((), (), s32[]{:S(2)}) async-start(), calls=%async_computation.2 | async-start | bytes 4456448 | tf_op jit(solution)/shard_map/all_gather | solution.py:76
  9.5 317.3 %all-gather.12.cloned.1.call-start = ((), (), s32[]{:S(2)}) async-start(), calls=%async_computation.4 | async-start | bytes 4456448 | tf_op jit(solution)/shard_map/all_gather | solution.py:81
  10.2 339.4 %all-reduce.5.cloned.1.call-start = ((), (), s32[]{:S(2)}) async-start(), calls=%async_computation | async-start | bytes 131072 | tf_op jit(solution)/shard_map/psum | solution.py:91
  12.0 527.7 %all-gather.10.cloned.1.call-start = ((), (), s32[]{:S(2)}) async-start(), calls=%async_computation.3 | async-start | bytes 8912896 | tf_op jit(solution)/shard_map/all_gather | solution.py:129
  231.6 103.3 %copy-start.7 = (u32[256]{0:T(256)S(1)}, u32[256]{0:T(256)}, u32[]{:S(2)}) copy-start(u32[256]{0:T(256)} %constant.50) | copy-start | bytes 3076
  231.6 104.5 %copy-start.6 = (s32[2]{0:T(128)S(1)}, s32[2]{0:T(128)}, u32[]{:S(2)}) copy-start(s32[2]{0:T(128)} %param.21) | copy-start | bytes 28
  231.6 119.0 %copy-start.3 = (bf16[256,512]{1,0:T(8,128)(2,1)S(1)}, bf16[256,512]{1,0:T(8,128)(2,1)}, u32[]{:S(2)}) copy-start(bf16[256,512]{1,0:T(8,128)(2,1)} %param.27) | copy-start | bytes 786436
  231.6 119.8 %copy-start.4 = (bf16[256,512]{1,0:T(8,128)(2,1)S(1)}, bf16[256,512]{1,0:T(8,128)(2,1)}, u32[]{:S(2)}) copy-start(bf16[256,512]{1,0:T(8,128)(2,1)} %param.25) | copy-start | bytes 786436
  231.7 120.7 %copy-start.5 = (bf16[256,512]{1,0:T(8,128)(2,1)S(1)}, bf16[256,512]{1,0:T(8,128)(2,1)}, u32[]{:S(2)}) copy-start(bf16[256,512]{1,0:T(8,128)(2,1)} %param.26) | copy-start | bytes 786436
  231.7 196.3 %copy-start.1 = (bf16[512,256]{1,0:T(8,128)(2,1)S(1)}, bf16[512,256]{1,0:T(8,128)(2,1)}, u32[]{:S(2)}) copy-start(bf16[512,256]{1,0:T(8,128)(2,1)} %param.28) | copy-start | bytes 786436
  231.7 476.2 %all-gather.14.cloned.1.call-start = ((), (), s32[]{:S(2)}) async-start(), calls=%async_computation.5 | async-start | bytes 8912896 | tf_op jit(solution)/shard_map/all_gather | solution.py:130
  719.3 5.8 copy-start.2
Sparse Core Ops, SparseCore 0:
  11.6 114.3 all-gather.5
  127.9 97.0 all-gather.7
  226.9 99.7 all-gather.11
  329.1 190.4 all-gather.9
  521.9 185.9 all-gather.13
Sparse Core Ops, SparseCore 1:
  16.2 313.5 all-reduce.4
where the time goes:
time: 947 us; the launch traced here: 938 us
  waiting for transfers between devices  462 us (49%)
  blocking collectives  396 us (42%)
  matrix products  33.6 us (4%)
  local copies, waits for them, and re-layouts  26.4 us (3%)
  between operations  16 us (2%)
    all_gather x1, waiting for transfers between devices, shards(): lax.all_gather(cross_values, 'pas', axis=0, tiled=True)  151 us
    all_gather x1, waiting for transfers between devices, shards(): whole_rows = lax.all_gather(passages, 'tp', axis=1, tiled=True)  114 us
    all_gather x3, blocking collectives, project_out(): return lax.all_gather(summed, 'pas', axis=1, tiled=True)  114 us
    all_gather x1, waiting for transfers between devices, shards(): lax.all_gather(w_key, 'pas', axis=0, tiled=True)  99 us
    all_gather x1, waiting for transfers between devices, shards(): lax.all_gather(w_value, 'pas', axis=0, tiled=True)  95 us
    psum x3, blocking collectives, project_out(): summed = lax.psum(term, 'tp')  82.5 us
    psum x1, blocking collectives, shards(): lax.psum((width_part(normed, w_gate), width_part(normed, w_up)), 'pas')  74.7 us
    psum x1, blocking collectives, shards(): lax.psum((width_part(normed, w_self_query), width_part(normed, w_self_key...  74.1 us
  transfers between devices with their start and end apart: 6, of which 4 were waited for; matrix products, arithmetic and copies ran while one was open for 4% of the time, Pallas kernels for 0%

commit v1 on v0

v1 whole, which is shorter than its diff:
```python
import jax
import jax.numpy as jnp
from jax import lax
from jax.experimental import pallas as pl
from jax.experimental.pallas import tpu as pltpu
from jax.sharding import PartitionSpec as P

BF = jnp.bfloat16
F32 = jnp.float32
MESH = pl.DeviceIdType.MESH
D = 4096
DH = 64
PLEN = 256
STEPS = 4
ROWS = 512
COLS = 512
OWN = 256
FFC = 1280
VROWS = 251
ACH = 4
WCH = 2
ARO = ROWS // ACH
WRO = OWN // WCH


def pack8(v):
    n = v.shape[1] // 2
    return jnp.concatenate([v[:, :n], v[:, n:]], axis=0)


def unpack8(p):
    return jnp.concatenate([p[:4], p[4:8]], axis=1)


def pack16(v):
    n = v.shape[1] // 4
    return jnp.concatenate([v[:, n * k : n * k + n] for k in range(4)], axis=0)


def unpack16(p):
    return jnp.concatenate([p[4 * k : 4 * k + 4] for k in range(4)], axis=1)


def pad8(v):
    return jnp.concatenate([v, jnp.zeros_like(v)], axis=0)


def head_mask():
    head = lax.broadcasted_iota(jnp.int32, (8, COLS), 0)
    lane = lax.broadcasted_iota(jnp.int32, (8, COLS), 1)
    return jnp.where((lane >= head * DH) & (lane < head * DH + DH), 1.0, 0.0).astype(F32)


def by_head(q):
    mask = head_mask()
    return jnp.concatenate([q[s : s + 1] * mask for s in range(STEPS)], axis=0).astype(BF)


def own_head(acc):
    mask = head_mask()
    rows = [
        jnp.sum(acc[8 * s : 8 * s + 8] * mask, axis=0, keepdims=True) for s in range(STEPS)
    ]
    return jnp.concatenate(rows, axis=0)


def attend(q, keys, values, live):
    scores = lax.dot_general(
        by_head(q), keys, (((1,), (1,)), ((), ())), preferred_element_type=F32
    ) * (1.0 / DH**0.5)
    scores = jnp.where(live, scores, -1e30)
    peak = jnp.max(scores, axis=1, keepdims=True)
    weights = jnp.where(live, jnp.exp(scores - peak), 0.0).astype(BF)
    total = jnp.sum(weights.astype(F32), axis=1, keepdims=True)
    accum = jnp.dot(weights, values, preferred_element_type=F32)
    return peak, total, accum


def split_sum(ss):
    hi = ss.astype(BF).astype(F32)
    lo = ss - hi
    z = jnp.zeros_like(ss)
    return jnp.broadcast_to(jnp.concatenate([hi, lo, z, z], axis=0), (16, 128))


def kernel(
    tok,
    lens,
    g_self,
    g_cross,
    g_ffn,
    passages,
    w_key,
    w_value,
    w_sq,
    w_sk,
    w_sv,
    w_so,
    w_cq,
    w_co,
    w_gate,
    w_up,
    w_down,
    emb,
    out,
    kout,
    vout,
    a_all,
    w_all,
    kv,
    emb_v,
    sq_v,
    sk_v,
    sv_v,
    so_v,
    cq_v,
    co_v,
    gate_v,
    up_v,
    down_v,
    s1a,
    r1a,
    r1b,
    r2,
    r3,
    r4,
    r5,
    r6,
    r7,
    r8,
    lsem,
    osem,
    az_r,
    ay_r,
    wz_r,
    wx_r,
    ws_r,
    big_s,
    es,
    er,
):
    pb = lax.axis_index("pb")
    pas = lax.axis_index("pas")
    tp = lax.axis_index("tp")
    x, zl = pas // 4, pas % 4
    zh, y = tp // 4, tp % 4
    xs = [(x + k) % 4 for k in range(4)]
    zs = [(zl + k) % 4 for k in range(4)]
    ys = [(y + k) % 4 for k in range(4)]
    xb = [(x - k + 4) % 4 for k in range(4)]
    zb = [(zl - k + 4) % 4 for k in range(4)]
    far = (2, 1, 3, 0)
    pas_peers = [
        (pb, xs[a] * 4 + zs[b], tp) for a in far for b in (3, 2, 1, 0) if (a, b) != (0, 0)
    ]
    tp_peers = [
        (pb, pas, (zh * 4 if b == 0 else (1 - zh) * 4) + ys[a])
        for b in (1, 0)
        for a in far
        if (a, b) != (0, 0)
    ]
    x_peers = {k: (pb, xs[k] * 4 + zl, tp) for k in (1, 3, 2)}
    z_peers = {k: (pb, x * 4 + zs[k], tp) for k in (1, 3, 2)}
    y_peers = {k: (pb, pas, zh * 4 + ys[k]) for k in (1, 3, 2)}
    z4_peer = (pb, pas, (1 - zh) * 4 + y)
    sibling = (1 - pb, pas, tp)

    pas0 = pl.multiple_of(pas * OWN, OWN)
    tp0 = pl.multiple_of(tp * COLS, COLS)
    loads = [
        (passages, a_all.at[:, pl.ds(tp0, COLS)]),
        (w_key, w_all.at[0, pl.ds(pas0, OWN)]),
        (w_value, w_all.at[1, pl.ds(pas0, OWN)]),
        (emb, emb_v),
        (w_sq, sq_v),
        (w_sk, sk_v),
        (w_sv, sv_v),
        (w_so, so_v),
        (w_cq, cq_v),
        (w_co, co_v),
        (w_gate, gate_v),
        (w_up, up_v),
        (w_down, down_v),
    ]
    local = [pltpu.make_async_copy(s, d, lsem.at[n]) for n, (s, d) in enumerate(loads)]
    for c in local:
        c.start()

    barrier = pltpu.get_barrier_semaphore()
    greet = pas_peers + tp_peers + [sibling]
    for d in greet:
        pl.semaphore_signal(barrier, inc=1, device_id=d, device_id_type=MESH)
    pl.semaphore_wait(barrier, len(greet))

    def send(src, dst, ssem, rsem, dev):
        pltpu.make_async_remote_copy(
            src_ref=src,
            dst_ref=dst,
            send_sem=ssem,
            recv_sem=rsem,
            device_id=dev,
            device_id_type=MESH,
        ).start()

    def wait_bytes(ref, sem):
        pltpu.make_async_copy(ref, ref, sem).wait()

    def a_piece(block, c):
        cols = pl.ds(pl.multiple_of(block * COLS, COLS), COLS)
        return a_all.at[pl.ds(c * ARO, ARO), cols]

    def w_piece(block, c):
        return w_all.at[pb, pl.ds(pl.multiple_of(block * OWN + c * WRO, WRO), WRO)]

    def a_send(block, c, peers, rsem):
        piece = a_piece(block, c)
        for p in peers:
            send(piece, piece, big_s.at[0], rsem, p)

    def w_sibling(block, c):
        piece = w_piece(block, c)
        send(piece, piece, big_s.at[2], ws_r.at[0], sibling)

    def w_to_x(block, kz, c):
        piece = w_piece(block, c)
        for k in (1, 3, 2):
            send(piece, piece, big_s.at[1], wx_r.at[k - 1, kz, c], x_peers[k])

    def w_from_z(kz):
        block = x * 4 + zb[kz]
        for c in range(WCH):
            wait_bytes(w_piece(block, c), wz_r.at[kz - 1, c])
            w_to_x(block, kz, c)
            w_sibling(block, c)

    def w_from_x(kx, kz):
        block = xb[kx] * 4 + zb[kz]
        for c in range(WCH):
            wait_bytes(w_piece(block, c), wx_r.at[kx - 1, kz, c])
            w_sibling(block, c)

    def a_from_z(c):
        block = (1 - zh) * 4 + y
        wait_bytes(a_piece(block, c), az_r.at[c])
        a_send(block, c, [y_peers[k] for k in (1, 3, 2)], ay_r.at[1])

    def spread(buf, me, peers, n):
        slot = buf.at[me]
        for p in peers:
            send(slot, slot, es.at[n], er.at[n], p)

    def collect(buf, count, n):
        wait_bytes(buf.at[pl.ds(0, count - 1)], er.at[n])

    def gain(g):
        return jnp.concatenate([g[pl.ds(2 * pas, 1), :], g[pl.ds(2 * pas + 1, 1), :]], axis=1)

    for n in range(3):
        local[n].wait()
    for c in range(WCH):
        piece = w_piece(pas, c)
        for k in (1, 3, 2):
            send(piece, piece, big_s.at[1], wz_r.at[k - 1, c], z_peers[k])
        w_to_x(pas, 0, c)
    for c in range(ACH):
        a_send(tp, c, [z4_peer], az_r.at[c])
        a_send(tp, c, [y_peers[k] for k in (1, 3, 2)], ay_r.at[0])

    local[3].wait()
    row = lax.broadcasted_iota(jnp.int32, (8, VROWS), 0)
    place = lax.broadcasted_iota(jnp.int32, (8, VROWS), 1) + (pas * 8 + tp) * VROWS
    wanted = jnp.full((8, VROWS), -1, jnp.int32)
    for s in range(STEPS):
        wanted = jnp.where(row == s, tok[s], wanted)
    onehot = jnp.where(place == wanted, 1.0, 0.0).astype(BF)
    mine = jnp.dot(onehot, emb_v[...], preferred_element_type=F32)
    for i in range(16):
        s1a[i] = pack8(mine[:4, OWN * i : OWN * i + OWN])
    r1a[pas] = s1a[pas]
    for p in pas_peers:
        send(s1a.at[p[1]], r1a.at[pas], es.at[0], er.at[0], p)

    w_from_z(1)

    collect(r1a, 16, 0)
    r1b[tp] = jnp.sum(r1a[...], axis=0)
    spread(r1b, tp, tp_peers, 1)

    w_from_z(3)
    a_from_z(0)

    collect(r1b, 8, 1)
    state0 = unpack8(jnp.sum(r1b[...], axis=0))

    def scaled(state, g):
        ss = jnp.sum(state * state, axis=1, keepdims=True)
        return pad8(state * gain(g)).astype(BF), ss

    def rms(ss):
        return lax.rsqrt(ss * (1.0 / D) + 1e-06)

    a, ss = scaled(state0, g_self)
    parts = []
    for n, w in ((4, sq_v), (5, sk_v), (6, sv_v)):
        local[n].wait()
        parts.append(pack16(jnp.dot(a, w[...], preferred_element_type=F32)[:4]))
    r2[pas] = jnp.concatenate(parts + [split_sum(ss)], axis=1).astype(BF)
    spread(r2, pas, pas_peers, 2)

    w_from_z(2)
    a_from_z(1)

    collect(r2, 16, 2)
    total = r2[0].astype(F32)
    for i in range(1, 16):
        total = total + r2[i].astype(F32)
    scale = rms(total[0:4, 384:385] + total[4:8, 384:385])
    q, k, v = [unpack16(total[:, 128 * n : 128 * n + 128]) * scale for n in range(3)]
    none = jnp.zeros((124, COLS), F32)
    keys = jnp.concatenate([k, none], axis=0).astype(BF)
    values = jnp.concatenate([v, none], axis=0).astype(BF)
    step = lax.broadcasted_iota(jnp.int32, (32, 128), 0)
    other = lax.broadcasted_iota(jnp.int32, (32, 128), 1)
    _, weight, accum = attend(q.astype(BF).astype(F32), keys, values, other * 8 <= step)
    heads = own_head(accum / weight)
    local[7].wait()
    r3[tp] = pack8(jnp.dot(pad8(heads).astype(BF), so_v[...], preferred_element_type=F32)[:4])
    spread(r3, tp, tp_peers, 3)

    a_from_z(2)
    for kx in (1, 3, 2):
        w_from_x(kx, 0)

    collect(r3, 8, 3)
    state1 = state0 + unpack8(jnp.sum(r3[...], axis=0))
    a, ss = scaled(state1, g_cross)
    local[8].wait()
    part = jnp.dot(a, cq_v[...], preferred_element_type=F32)[:4]
    r4[pas] = jnp.concatenate([pack8(part), jnp.broadcast_to(pad8(ss), (8, 128))], axis=1)
    spread(r4, pas, pas_peers, 4)

    a_from_z(3)
    for kz in (1, 3, 2):
        for kx in (1, 3, 2):
            w_from_x(kx, kz)

    collect(r4, 16, 4)
    total = jnp.sum(r4[...], axis=0)
    cquery = unpack8(total[:, :256]) * rms(total[:4, 256:257])

    wait_bytes(a_all.at[:, pl.ds(0, 3 * COLS)], ay_r.at[0])
    wait_bytes(a_all.at[:, pl.ds(0, 3 * COLS)], ay_r.at[1])
    wait_bytes(w_all.at[0, pl.ds(0, 15 * OWN)], ws_r.at[0])
    for c in range(2):

        def tile(n, carry):
            cols = pl.ds(pl.multiple_of(n * 256, 256), 256)
            kv[c, :, cols] = jnp.dot(
                a_all[...], w_all[c, :, cols], preferred_element_type=F32
            ).astype(BF)
            return carry

        lax.fori_loop(0, 2, tile, 0)
    outs = [
        pltpu.make_async_copy(kv.at[0], kout, osem.at[0]),
        pltpu.make_async_copy(kv.at[1], vout, osem.at[1]),
    ]
    for c in outs:
        c.start()

    slot = lax.broadcasted_iota(jnp.int32, (32, ROWS), 1)
    live = (slot < lens[0]) | ((slot >= PLEN) & (slot < lens[1] + PLEN))
    peak, weight, accum = attend(cquery.astype(BF).astype(F32), kv[0], kv[1], live)
    head = lax.broadcasted_iota(jnp.int32, (8, 128), 0)
    lane = lax.broadcasted_iota(jnp.int32, (8, 128), 1)
    rows = []
    for g in range(2):
        for s in range(STEPS):
            both = jnp.where(lane == head - 4 * g, peak[8 * s : 8 * s + 8], 0.0) + jnp.where(
                (lane >= 64) & (lane - 64 == head - 4 * g), weight[8 * s : 8 * s + 8], 0.0
            )
            rows.append(jnp.sum(both, axis=0, keepdims=True))
    r5[pas] = jnp.concatenate([pack8(own_head(accum)), jnp.concatenate(rows, axis=0)], axis=1)
    spread(r5, pas, pas_peers, 5)
    collect(r5, 16, 5)
    peaks = [r5[i, :, 256:384] for i in range(16)]
    top = peaks[0]
    for i in range(1, 16):
        top = jnp.maximum(top, peaks[i])
    shares = []
    weight = jnp.zeros((8, 128), F32)
    for i in range(16):
        share = jnp.where(lane < 4, jnp.exp(peaks[i] - top), 0.0)
        weight = weight + share * pltpu.roll(peaks[i], 64, 1)
        shares.append(share)
    inv = 1.0 / jnp.where(lane < 4, weight, 1.0)
    shares = jnp.concatenate([s * inv for s in shares], axis=0)
    lane_of = lax.broadcasted_iota(jnp.int32, (128, 256), 0)
    column = lax.broadcasted_iota(jnp.int32, (128, 256), 1)
    widen = jnp.where((column >= lane_of * DH) & (column < lane_of * DH + DH), 1.0, 0.0)
    wide = jnp.dot(
        shares, widen.astype(F32), preferred_element_type=F32, precision=lax.Precision.HIGHEST
    )
    mixed = jnp.zeros((8, 256), F32)
    for i in range(16):
        mixed = mixed + wide[8 * i : 8 * i + 8] * r5[i, :, :256]
    local[9].wait()
    heads = pad8(unpack8(mixed)).astype(BF)
    r6[tp] = pack8(jnp.dot(heads, co_v[...], preferred_element_type=F32)[:4])
    spread(r6, tp, tp_peers, 6)
    collect(r6, 8, 6)
    state2 = state1 + unpack8(jnp.sum(r6[...], axis=0))

    a, ss = scaled(state2, g_ffn)
    local[10].wait()
    local[11].wait()
    gated = jnp.dot(a, gate_v[...], preferred_element_type=F32)[:4]
    upper = jnp.dot(a, up_v[...], preferred_element_type=F32)[:4]
    r7[pas] = jnp.concatenate(
        [pack16(jnp.concatenate([gated, upper], axis=1)), split_sum(ss)], axis=1
    ).astype(BF)
    spread(r7, pas, pas_peers, 7)
    collect(r7, 16, 7)
    total = r7[0].astype(F32)
    for i in range(1, 16):
        total = total + r7[i].astype(F32)
    scale = rms(total[0:4, 640:641] + total[4:8, 640:641])
    scale = jnp.concatenate([scale, scale], axis=0)
    gated = total[0:8, :640] * scale
    upper = total[8:16, :640] * scale
    gelu = 0.5 * gated * (1.0 + jnp.tanh(0.7978845608028654 * (gated + 0.044715 * gated * gated * gated)))
    hidden = (gelu * upper).astype(BF)
    local[12].wait()
    low = jnp.dot(hidden, down_v[0:640], preferred_element_type=F32)
    high = jnp.dot(hidden, down_v[640:1280], preferred_element_type=F32)
    r8[tp] = pack8(low[:4] + high[4:8])
    spread(r8, tp, tp_peers, 8)
    collect(r8, 8, 8)
    whole = state2 + unpack8(jnp.sum(r8[...], axis=0))
    own = whole[:, 0:32]
    for t in range(1, 8):
        own = jnp.where(tp == t, whole[:, 32 * t : 32 * t + 32], own)
    out[...] = own

    for n, (buf, count) in enumerate(
        ((r1a, 16), (r1b, 8), (r2, 16), (r3, 8), (r4, 16), (r5, 16), (r6, 8), (r7, 16), (r8, 8))
    ):
        wait_bytes(buf.at[pl.ds(0, count - 1)], es.at[n])
    wait_bytes(a_all.at[:, pl.ds(0, 7 * COLS)], big_s.at[0])
    wait_bytes(w_all.at[0, pl.ds(0, 15 * OWN)], big_s.at[1])
    wait_bytes(w_all.at[0, pl.ds(0, 15 * OWN)], big_s.at[2])
    for c in outs:
        c.wait()


def shards(
    token_ids,
    embedding,
    passages,
    passage_lengths,
    w_key,
    w_value,
    norm_self,
    w_self_query,
    w_self_key,
    w_self_value,
    w_self_out,
    norm_cross,
    w_cross_query,
    w_cross_out,
    norm_ffn,
    w_gate,
    w_up,
    w_down,
):
    smem = pl.BlockSpec(memory_space=pltpu.SMEM)
    vmem = pl.BlockSpec(memory_space=pltpu.VMEM)
    hbm = pl.BlockSpec(memory_space=pltpu.HBM)
    dma = pltpu.SemaphoreType.DMA
    return pl.pallas_call(
        kernel,
        name="decoder_layer",
        out_shape=(
            jax.ShapeDtypeStruct((STEPS, 32), F32),
            jax.ShapeDtypeStruct((ROWS, COLS), BF),
            jax.ShapeDtypeStruct((ROWS, COLS), BF),
        ),
        in_specs=[smem, smem, vmem, vmem, vmem] + [hbm] * 13,
        out_specs=(vmem, hbm, hbm),
        scratch_shapes=[
            pltpu.VMEM((ROWS, D), BF),
            pltpu.VMEM((2, D, COLS), BF),
            pltpu.VMEM((2, ROWS, COLS), BF),
            pltpu.VMEM((VROWS, D), BF),
            pltpu.VMEM((OWN, COLS), BF),
            pltpu.VMEM((OWN, COLS), BF),
            pltpu.VMEM((OWN, COLS), BF),
            pltpu.VMEM((COLS, OWN), BF),
            pltpu.VMEM((OWN, COLS), BF),
            pltpu.VMEM((COLS, OWN), BF),
            pltpu.VMEM((OWN, FFC), BF),
            pltpu.VMEM((OWN, FFC), BF),
            pltpu.VMEM((FFC, OWN), BF),
            pltpu.VMEM((16, 8, 128), F32),
            pltpu.VMEM((16, 8, 128), F32),
            pltpu.VMEM((8, 8, 128), F32),
            pltpu.VMEM((16, 16, 512), BF),
            pltpu.VMEM((8, 8, 128), F32),
            pltpu.VMEM((16, 8, 384), F32),
            pltpu.VMEM((16, 8, 384), F32),
            pltpu.VMEM((8, 8, 128), F32),
            pltpu.VMEM((16, 16, 768), BF),
            pltpu.VMEM((8, 8, 128), F32),
            dma((13,)),
            dma((2,)),
            dma((ACH,)),
            dma((2,)),
            dma((3, WCH)),
            dma((3, 4, WCH)),
            dma((1,)),
            dma((3,)),
            dma((9,)),
            dma((9,)),
        ],
        compiler_params=pltpu.CompilerParams(
            collective_id=1, has_side_effects=True, vmem_limit_bytes=56 << 20
        ),
        cost_estimate=pl.CostEstimate(
            flops=2 * 2 * ROWS * COLS * D, bytes_accessed=16 << 20, transcendentals=1 << 20
        ),
    )(
        token_ids,
        passage_lengths,
        norm_self.reshape(32, 128),
        norm_cross.reshape(32, 128),
        norm_ffn.reshape(32, 128),
        passages,
        w_key,
        w_value,
        w_self_query,
        w_self_key,
        w_self_value,
        w_self_out,
        w_cross_query,
        w_cross_out,
        w_gate,
        w_up,
        w_down,
        embedding,
    )


def solution(mesh):
    in_specs = (
        P("pb"),
        P(("pas", "tp"), None),
        P(("pb", "pas"), "tp"),
        P(("pb", "pas")),
        P("pas", "tp"),
        P("pas", "tp"),
        P(),
        P("pas", "tp"),
        P("pas", "tp"),
        P("pas", "tp"),
        P("tp", "pas"),
        P(),
        P("pas", "tp"),
        P("tp", "pas"),
        P(),
        P("pas", "tp"),
        P("pas", "tp"),
        P("tp", "pas"),
    )
    out_specs = (P("pb", ("pas", "tp")), P(("pb", "pas"), "tp"), P(("pb", "pas"), "tp"))
    return jax.shard_map(shards, mesh=mesh, in_specs=in_specs, out_specs=out_specs, check_vma=False)
```

time: 947 us -> 132 us (0.14)
  waiting for transfers between devices: 462 us -> 0 us
  blocking collectives: 396 us -> 0 us
  Pallas kernels: 0 us -> 127 us
  matrix products: 33.6 us -> 0 us
  local copies, waits for them, and re-layouts: 26.4 us -> 4.99 us
  between operations: 16 us -> 0.65 us
    all_gather x5 -> x0, waiting for transfers between devices: 459 us -> none  [the longest x1 151 us: shards(): lax.all_gather(cross_values, 'pas', axis=0, tiled=True)]
    psum x6 -> x0, blocking collectives: 270 us -> none  [the longest x3 82.5 us: project_out(): summed = lax.psum(term, 'tp')]
    pallas_call x0 -> x1, Pallas kernels: none -> 127 us  [shards(): pl.pallas_call(kernel, name='decoder_layer', out_shape=(jax.ShapeDtypeStr...]
    all_gather x3 -> x0, blocking collectives: 114 us -> none  [project_out(): return lax.all_gather(summed, 'pas', axis=1, tiled=True)]
    dot_general x15 -> x0, matrix products: 33.5 us -> none  [the longest x1 6.59 us: shards(): jnp.dot(whole_rows, lax.all_gather(w_value, 'pas', axis=0, tiled=True), p...]
    all_gather x2 -> x0, local copies, waits for them, and re-layouts: 22.7 us -> none  [the longest x1 11.4 us: shards(): lax.all_gather(cross_values, 'pas', axis=0, tiled=True)]
    unnamed x1 -> x0, blocking collectives: 12.3 us -> none
  transfers between devices with their start and end apart: 6 -> 0, of which waited for: 4 -> 0; matrix products, arithmetic and copies ran while one was open for 4% -> 0% of each run, Pallas kernels for 0% -> 0%
where the time goes in v1:
time: 132 us
  Pallas kernels  127 us (96%)
  local copies, waits for them, and re-layouts  4.99 us (4%)
    pallas_call x1, Pallas kernels, shards(): pl.pallas_call(kernel, name='decoder_layer', out_shape=(jax.ShapeDtypeStr...  127 us
    unnamed x3, local copies, waits for them, and re-layouts  4.99 us

profile of v1, /device:TPU:6, one launch (start us, length us, event | category | flops | bytes accessed | tf_op | source)
XLA Modules:
  0.0 132.1 jit_solution(5499575022999390892)
XLA Ops:
  0.6 126.5 %decoder_layer.1 = (f32[4,32]{1,0:T(4,128)}, bf16[512,512]{1,0:T(8,128)(2,1)}, bf16[512,512]{1,0:T(8,128)(2,1)}) custom-call(s32[4]{0:T(128)} %tok.1, s32[2]{0:T(128)} %lens.1, f32[32,128]{1,0:T(8,128)} %bitcast.3, f32[32,128]{1,0:T(8,128)} %bitcast.4, f32[32,128]{1,0:T(8,128)} %bitcast.5, bf16[512,512]{1,0:T(8,128)(2,1)} %passages.1, ...), custom_call_target="tpu_custom_call" | custom-call | flops 4294967296 | bytes 16777216 | tf_op jit(solution)/shard_map/decoder_layer/pallas_call | solution.py:480
  127.2 1.3 copy.24
  128.4 1.9 %copy.25 = bf16[512,512]{1,0:T(8,128)(2,1)} copy(bf16[512,512]{1,0:T(8,128)(2,1)} %get-tuple-element.7) | data formatting | bytes 1048576
  130.3 1.9 %copy.26 = bf16[512,512]{1,0:T(8,128)(2,1)} copy(bf16[512,512]{1,0:T(8,128)(2,1)} %get-tuple-element.8) | data formatting | bytes 1048576

commit v2 on v1

--- a/solution.py
+++ b/solution.py
@@ -21,6 +21,8 @@
 WCH = 2
 ARO = ROWS // ACH
 WRO = OWN // WCH
+PASSED = ((1, 0), (3, 1))
+KEPT = ((1, 1), (3, 0), (2, 0), (2, 1))
 
 
 def pack8(v):
@@ -122,8 +124,10 @@
     r1a,
     r1b,
     r2,
+    r2z,
     r3,
     r4,
+    r4z,
     r5,
     r6,
     r7,
@@ -131,7 +135,8 @@
     lsem,
     osem,
     az_r,
-    ay_r,
+    af_r,
+    an_r,
     wz_r,
     wx_r,
     ws_r,
@@ -149,6 +154,7 @@
     ys = [(y + k) % 4 for k in range(4)]
     xb = [(x - k + 4) % 4 for k in range(4)]
     zb = [(zl - k + 4) % 4 for k in range(4)]
+    yb = [(y - k + 4) % 4 for k in range(4)]
     far = (2, 1, 3, 0)
     pas_peers = [
         (pb, xs[a] * 4 + zs[b], tp) for a in far for b in (3, 2, 1, 0) if (a, b) != (0, 0)
@@ -190,7 +196,6 @@
     greet = pas_peers + tp_peers + [sibling]
     for d in greet:
         pl.semaphore_signal(barrier, inc=1, device_id=d, device_id_type=MESH)
-    pl.semaphore_wait(barrier, len(greet))
 
     def send(src, dst, ssem, rsem, dev):
         pltpu.make_async_remote_copy(
@@ -212,10 +217,27 @@
     def w_piece(block, c):
         return w_all.at[pb, pl.ds(pl.multiple_of(block * OWN + c * WRO, WRO), WRO)]
 
-    def a_send(block, c, peers, rsem):
+    def a_to_z(c):
+        piece = a_piece(tp, c)
+        send(piece, piece, big_s.at[0], az_r.at[c], z4_peer)
+
+    def a_to_y(half, block, c):
         piece = a_piece(block, c)
-        for p in peers:
-            send(piece, piece, big_s.at[0], rsem, p)
+        for k, passed_on in ((1, c % 2 == 0), (3, c % 2 == 1)):
+            rsem = af_r.at[half, c] if passed_on else an_r.at[half]
+            send(piece, piece, big_s.at[0], rsem, y_peers[k])
+
+    def a_from_z(c):
+        block = (1 - zh) * 4 + y
+        wait_bytes(a_piece(block, c), az_r.at[c])
+        a_to_y(1, block, c)
+
+    def a_from_y(half, c):
+        k = 1 if c % 2 == 0 else 3
+        block = (zh if half == 0 else 1 - zh) * 4 + yb[k]
+        piece = a_piece(block, c)
+        wait_bytes(piece, af_r.at[half, c])
+        send(piece, piece, big_s.at[0], an_r.at[half], y_peers[k])
 
     def w_sibling(block, c):
         piece = w_piece(block, c)
@@ -223,8 +245,13 @@
 
     def w_to_x(block, kz, c):
         piece = w_piece(block, c)
-        for k in (1, 3, 2):
+        for k in (1, 3):
             send(piece, piece, big_s.at[1], wx_r.at[k - 1, kz, c], x_peers[k])
+
+    def w_to_z(k):
+        for c in range(WCH):
+            piece = w_piece(pas, c)
+            send(piece, piece, big_s.at[1], wz_r.at[k - 1, c], z_peers[k])
 
     def w_from_z(kz):
         block = x * 4 + zb[kz]
@@ -233,16 +260,14 @@
             w_to_x(block, kz, c)
             w_sibling(block, c)
 
-    def w_from_x(kx, kz):
-        block = xb[kx] * 4 + zb[kz]
-        for c in range(WCH):
-            wait_bytes(w_piece(block, c), wx_r.at[kx - 1, kz, c])
+    def w_from_x(kz, pieces):
+        for kx, c in pieces:
+            block = xb[kx] * 4 + zb[kz]
+            piece = w_piece(block, c)
+            wait_bytes(piece, wx_r.at[kx - 1, kz, c])
+            if (kx, c) in PASSED:
+                send(piece, piece, big_s.at[1], wx_r.at[1, kz, c], x_peers[kx])
             w_sibling(block, c)
-
-    def a_from_z(c):
-        block = (1 - zh) * 4 + y
-        wait_bytes(a_piece(block, c), az_r.at[c])
-        a_send(block, c, [y_peers[k] for k in (1, 3, 2)], ay_r.at[1])
 
     def spread(buf, me, peers, n):
         slot = buf.at[me]
@@ -252,19 +277,23 @@
     def collect(buf, count, n):
         wait_bytes(buf.at[pl.ds(0, count - 1)], er.at[n])
 
+    def merge_pas(part, bx, bz, n):
+        bx[x] = part
+        for k in (2, 1, 3):
+            send(bx.at[x], bx.at[x], es.at[n], er.at[n], x_peers[k])
+
+    def merge_pas_z(bx, bz, n):
+        wait_bytes(bx.at[pl.ds(0, 3)], er.at[n])
+        bz[zl] = bx[0] + bx[1] + bx[2] + bx[3]
+        for k in (3, 2, 1):
+            send(bz.at[zl], bz.at[zl], es.at[n + 7], er.at[n + 7], z_peers[k])
+
+    def merged(bz, n):
+        wait_bytes(bz.at[pl.ds(0, 3)], er.at[n + 7])
+        return bz[0] + bz[1] + bz[2] + bz[3]
+
     def gain(g):
         return jnp.concatenate([g[pl.ds(2 * pas, 1), :], g[pl.ds(2 * pas + 1, 1), :]], axis=1)
-
-    for n in range(3):
-        local[n].wait()
-    for c in range(WCH):
-        piece = w_piece(pas, c)
-        for k in (1, 3, 2):
-            send(piece, piece, big_s.at[1], wz_r.at[k - 1, c], z_peers[k])
-        w_to_x(pas, 0, c)
-    for c in range(ACH):
-        a_send(tp, c, [z4_peer], az_r.at[c])
-        a_send(tp, c, [y_peers[k] for k in (1, 3, 2)], ay_r.at[0])
 
     local[3].wait()
     row = lax.broadcasted_iota(jnp.int32, (8, VROWS), 0)
@@ -277,17 +306,33 @@
     for i in range(16):
         s1a[i] = pack8(mine[:4, OWN * i : OWN * i + OWN])
     r1a[pas] = s1a[pas]
+    pl.semaphore_wait(barrier, len(greet))
     for p in pas_peers:
         send(s1a.at[p[1]], r1a.at[pas], es.at[0], er.at[0], p)
 
+    for n in range(3):
+        local[n].wait()
+    for c in range(WCH):
+        w_to_x(pas, 0, c)
+    w_to_z(1)
+    a_to_z(0)
+    for c in range(ACH):
+        a_to_y(0, tp, c)
+
+    w_from_x(0, PASSED)
     w_from_z(1)
+    w_to_z(3)
 
     collect(r1a, 16, 0)
     r1b[tp] = jnp.sum(r1a[...], axis=0)
     spread(r1b, tp, tp_peers, 1)
 
-    w_from_z(3)
+    a_from_y(0, 0)
+    a_from_y(0, 1)
     a_from_z(0)
+    a_to_z(1)
+    w_from_x(1, PASSED)
+    w_from_x(0, KEPT)
 
     collect(r1b, 8, 1)
     state0 = unpack8(jnp.sum(r1b[...], axis=0))
@@ -303,19 +348,25 @@
     parts = []
     for n, w in ((4, sq_v), (5, sk_v), (6, sv_v)):
         local[n].wait()
-        parts.append(pack16(jnp.dot(a, w[...], preferred_element_type=F32)[:4]))
-    r2[pas] = jnp.concatenate(parts + [split_sum(ss)], axis=1).astype(BF)
-    spread(r2, pas, pas_peers, 2)
-
-    w_from_z(2)
+        parts.append(pack8(jnp.dot(a, w[...], preferred_element_type=F32)[:4]))
+    parts.append(jnp.broadcast_to(pad8(ss), (8, 128)))
+    merge_pas(jnp.concatenate(parts, axis=1), r2, r2z, 2)
+
+    a_from_y(0, 2)
+    a_from_y(0, 3)
+    w_from_z(3)
+    w_to_z(2)
+    merge_pas_z(r2, r2z, 2)
+
+    a_from_y(1, 0)
     a_from_z(1)
-
-    collect(r2, 16, 2)
-    total = r2[0].astype(F32)
-    for i in range(1, 16):
-        total = total + r2[i].astype(F32)
-    scale = rms(total[0:4, 384:385] + total[4:8, 384:385])
-    q, k, v = [unpack16(total[:, 128 * n : 128 * n + 128]) * scale for n in range(3)]
+    a_to_z(2)
+    w_from_x(3, PASSED)
+    w_from_x(1, KEPT)
+
+    total = merged(r2z, 2)
+    scale = rms(total[:4, 768:769])
+    q, k, v = [unpack8(total[:, 256 * n : 256 * n + 256]) * scale for n in range(3)]
     none = jnp.zeros((124, COLS), F32)
     keys = jnp.concatenate([k, none], axis=0).astype(BF)
     values = jnp.concatenate([v, none], axis=0).astype(BF)
@@ -327,29 +378,29 @@
     r3[tp] = pack8(jnp.dot(pad8(heads).astype(BF), so_v[...], preferred_element_type=F32)[:4])
     spread(r3, tp, tp_peers, 3)
 
+    a_from_y(1, 1)
+    w_from_z(2)
     a_from_z(2)
-    for kx in (1, 3, 2):
-        w_from_x(kx, 0)
+    a_to_z(3)
 
     collect(r3, 8, 3)
     state1 = state0 + unpack8(jnp.sum(r3[...], axis=0))
     a, ss = scaled(state1, g_cross)
     local[8].wait()
     part = jnp.dot(a, cq_v[...], preferred_element_type=F32)[:4]
-    r4[pas] = jnp.concatenate([pack8(part), jnp.broadcast_to(pad8(ss), (8, 128))], axis=1)
-    spread(r4, pas, pas_peers, 4)
-
+    part = jnp.concatenate([pack8(part), jnp.broadcast_to(pad8(ss), (8, 128))], axis=1)
+    merge_pas(part, r4, r4z, 4)
+
+    w_from_x(2, PASSED)
+    w_from_x(3, KEPT)
+    a_from_y(1, 2)
+    merge_pas_z(r4, r4z, 4)
     a_from_z(3)
-    for kz in (1, 3, 2):
-        for kx in (1, 3, 2):
-            w_from_x(kx, kz)
-
-    collect(r4, 16, 4)
-    total = jnp.sum(r4[...], axis=0)
-    cquery = unpack8(total[:, :256]) * rms(total[:4, 256:257])
-
-    wait_bytes(a_all.at[:, pl.ds(0, 3 * COLS)], ay_r.at[0])
-    wait_bytes(a_all.at[:, pl.ds(0, 3 * COLS)], ay_r.at[1])
+    w_from_x(2, KEPT)
+    a_from_y(1, 3)
+
+    for half in range(2):
+        wait_bytes(a_all.at[:, pl.ds(0, 2 * COLS)], an_r.at[half])
     wait_bytes(w_all.at[0, pl.ds(0, 15 * OWN)], ws_r.at[0])
     for c in range(2):
 
@@ -367,6 +418,9 @@
     ]
     for c in outs:
         c.start()
+
+    total = merged(r4z, 4)
+    cquery = unpack8(total[:, :256]) * rms(total[:4, 256:257])
 
     slot = lax.broadcasted_iota(jnp.int32, (32, ROWS), 1)
     live = (slot < lens[0]) | ((slot >= PLEN) & (slot < lens[1] + PLEN))
@@ -442,8 +496,18 @@
         own = jnp.where(tp == t, whole[:, 32 * t : 32 * t + 32], own)
     out[...] = own
 
-    for n, (buf, count) in enumerate(
-        ((r1a, 16), (r1b, 8), (r2, 16), (r3, 8), (r4, 16), (r5, 16), (r6, 8), (r7, 16), (r8, 8))
+    for n, buf, count in (
+        (0, r1a, 16),
+        (1, r1b, 8),
+        (2, r2, 4),
+        (9, r2z, 4),
+        (3, r3, 8),
+        (4, r4, 4),
+        (11, r4z, 4),
+        (5, r5, 16),
+        (6, r6, 8),
+        (7, r7, 16),
+        (8, r8, 8),
     ):
         wait_bytes(buf.at[pl.ds(0, count - 1)], es.at[n])
     wait_bytes(a_all.at[:, pl.ds(0, 7 * COLS)], big_s.at[0])
@@ -451,6 +515,12 @@
     wait_bytes(w_all.at[0, pl.ds(0, 15 * OWN)], big_s.at[2])
     for c in outs:
         c.wait()
+
+
+def finish(out_a, k_a, v_a, out_b, k_b, v_b):
+    out_b[...] = out_a[...]
+    k_b[...] = k_a[...]
+    v_b[...] = v_a[...]
 
 
 def shards(
@@ -477,7 +547,7 @@
     vmem = pl.BlockSpec(memory_space=pltpu.VMEM)
     hbm = pl.BlockSpec(memory_space=pltpu.HBM)
     dma = pltpu.SemaphoreType.DMA
-    return pl.pallas_call(
+    results = pl.pallas_call(
         kernel,
         name="decoder_layer",
         out_shape=(
@@ -504,9 +574,11 @@
             pltpu.VMEM((16, 8, 128), F32),
             pltpu.VMEM((16, 8, 128), F32),
             pltpu.VMEM((8, 8, 128), F32),
-            pltpu.VMEM((16, 16, 512), BF),
+            pltpu.VMEM((4, 8, 896), F32),
+            pltpu.VMEM((4, 8, 896), F32),
             pltpu.VMEM((8, 8, 128), F32),
-            pltpu.VMEM((16, 8, 384), F32),
+            pltpu.VMEM((4, 8, 384), F32),
+            pltpu.VMEM((4, 8, 384), F32),
             pltpu.VMEM((16, 8, 384), F32),
             pltpu.VMEM((8, 8, 128), F32),
             pltpu.VMEM((16, 16, 768), BF),
@@ -514,13 +586,14 @@
             dma((13,)),
             dma((2,)),
             dma((ACH,)),
+            dma((2, ACH)),
             dma((2,)),
             dma((3, WCH)),
             dma((3, 4, WCH)),
             dma((1,)),
             dma((3,)),
-            dma((9,)),
-            dma((9,)),
+            dma((12,)),
+            dma((12,)),
         ],
         compiler_params=pltpu.CompilerParams(
             collective_id=1, has_side_effects=True, vmem_limit_bytes=56 << 20
@@ -548,6 +621,14 @@
         w_down,
         embedding,
     )
+    return pl.pallas_call(
+        finish,
+        name="finish",
+        out_shape=tuple(jax.ShapeDtypeStruct(r.shape, r.dtype) for r in results),
+        in_specs=[vmem] * 3,
+        out_specs=(vmem, vmem, vmem),
+        compiler_params=pltpu.CompilerParams(vmem_limit_bytes=56 << 20),
+    )(*results)
 
 
 def solution(mesh):

time: 132 us -> 115 us (0.87)
  Pallas kernels: 127 us -> 114 us
  local copies, waits for them, and re-layouts: 4.99 us -> 0 us
    pallas_call x1, Pallas kernels: 127 us -> 112 us  [shards(): pl.pallas_call(kernel, name='decoder_layer', out_shape=(jax.ShapeDtypeStr...]
    unnamed x3 -> x0, local copies, waits for them, and re-layouts: 4.99 us -> none
    pallas_call x0 -> x1, Pallas kernels: none -> 2.21 us  [shards(): pl.pallas_call(finish, name='finish', out_shape=tuple((jax.ShapeDtypeStru...]
where the time goes in v2:
time: 115 us
  Pallas kernels  114 us (99%)
    pallas_call x1, Pallas kernels, shards(): pl.pallas_call(kernel, name='decoder_layer', out_shape=(jax.ShapeDtypeStr...  112 us

profile of v2, /device:TPU:6, one launch (start us, length us, event | category | flops | bytes accessed | tf_op | source)
XLA Modules:
  0.0 114.6 jit_solution(14571653937018750395)
XLA Ops:
  0.6 111.8 %decoder_layer.1 = (f32[4,32]{1,0:T(4,128)}, bf16[512,512]{1,0:T(8,128)(2,1)}, bf16[512,512]{1,0:T(8,128)(2,1)}) custom-call(s32[4]{0:T(128)} %tok.1, s32[2]{0:T(128)} %lens.1, f32[32,128]{1,0:T(8,128)} %bitcast.3, f32[32,128]{1,0:T(8,128)} %bitcast.4, f32[32,128]{1,0:T(8,128)} %bitcast.5, bf16[512,512]{1,0:T(8,128)(2,1)} %passages.1, ...), custom_call_target="tpu_custom_call" | custom-call | flops 4294967296 | bytes 16777216 | tf_op jit(solution)/shard_map/decoder_layer/pallas_call | solution.py:550
  112.4 2.2 %finish.1 = (f32[4,32]{1,0:T(4,128)}, bf16[512,512]{1,0:T(8,128)(2,1)}, bf16[512,512]{1,0:T(8,128)(2,1)}) custom-call(f32[4,32]{1,0:T(4,128)} %get-tuple-element.6.out_a, bf16[512,512]{1,0:T(8,128)(2,1)} %get-tuple-element.7.k_a, bf16[512,512]{1,0:T(8,128)(2,1)} %get-tuple-element.8.v_a), custom_call_target="tpu_custom_call" | custom-call | tf_op jit(solution)/shard_map/finish/pallas_call | solution.py:624

commit v3 on v2

--- a/solution.py
+++ b/solution.py
@@ -23,6 +23,17 @@
 WRO = OWN // WCH
 PASSED = ((1, 0), (3, 1))
 KEPT = ((1, 1), (3, 0), (2, 0), (2, 1))
+HALF = D // 2
+
+SCHEDULE = (
+    ("sz", 0), ("sy",), ("wp", 0), ("sz", 1), ("wz", 1), ("wz", 4), ("c1",),
+    ("ay", 0, 0), ("ay", 0, 1), ("az", 0), ("sz", 2), ("wp", 1), ("wp", 4), ("wk", 0), ("c2",),
+    ("ay", 0, 2), ("ay", 0, 3), ("wz", 2), ("wz", 5), ("c2z",),
+    ("ay", 1, 0), ("az", 1), ("sz", 3), ("wp", 2), ("wp", 5), ("wk", 1), ("wk", 4), ("c3",),
+    ("ay", 1, 1), ("wz", 3), ("wz", 6), ("az", 2), ("c4",),
+    ("wp", 3), ("wp", 6), ("wk", 2), ("wk", 5), ("ay", 1, 2), ("c4z",),
+    ("az", 3), ("wk", 3), ("wk", 6), ("ay", 1, 3), ("mm",), ("mm", 0), ("mm", 1), ("c5",),
+)
 
 
 def pack8(v):
@@ -110,6 +121,7 @@
     a_all,
     w_all,
     kv,
+    sums,
     emb_v,
     sq_v,
     sk_v,
@@ -224,7 +236,7 @@
     def a_to_y(half, block, c):
         piece = a_piece(block, c)
         for k, passed_on in ((1, c % 2 == 0), (3, c % 2 == 1)):
-            rsem = af_r.at[half, c] if passed_on else an_r.at[half]
+            rsem = af_r.at[half, c] if passed_on else an_r.at[half, c]
             send(piece, piece, big_s.at[0], rsem, y_peers[k])
 
     def a_from_z(c):
@@ -237,37 +249,62 @@
         block = (zh if half == 0 else 1 - zh) * 4 + yb[k]
         piece = a_piece(block, c)
         wait_bytes(piece, af_r.at[half, c])
-        send(piece, piece, big_s.at[0], an_r.at[half], y_peers[k])
+        send(piece, piece, big_s.at[0], an_r.at[half, c], y_peers[k])
 
     def w_sibling(block, c):
         piece = w_piece(block, c)
         send(piece, piece, big_s.at[2], ws_r.at[0], sibling)
 
-    def w_to_x(block, kz, c):
+    def w_to_x(block, e, c):
         piece = w_piece(block, c)
         for k in (1, 3):
-            send(piece, piece, big_s.at[1], wx_r.at[k - 1, kz, c], x_peers[k])
-
-    def w_to_z(k):
-        for c in range(WCH):
-            piece = w_piece(pas, c)
-            send(piece, piece, big_s.at[1], wz_r.at[k - 1, c], z_peers[k])
-
-    def w_from_z(kz):
-        block = x * 4 + zb[kz]
-        for c in range(WCH):
-            wait_bytes(w_piece(block, c), wz_r.at[kz - 1, c])
-            w_to_x(block, kz, c)
-            w_sibling(block, c)
-
-    def w_from_x(kz, pieces):
-        for kx, c in pieces:
-            block = xb[kx] * 4 + zb[kz]
-            piece = w_piece(block, c)
-            wait_bytes(piece, wx_r.at[kx - 1, kz, c])
-            if (kx, c) in PASSED:
-                send(piece, piece, big_s.at[1], wx_r.at[1, kz, c], x_peers[kx])
-            w_sibling(block, c)
+            send(piece, piece, big_s.at[1], wx_r.at[k - 1, e, c], x_peers[k])
+
+    def w_to_z(block, up, n, c):
+        piece = w_piece(block, c)
+
+        @pl.when(zl < 3 if up else zl > 0)
+        def _():
+            to = (pb, pas + 1, tp) if up else (pb, pas - 1, tp)
+            send(piece, piece, big_s.at[3], wz_r.at[n if up else n + 3, c], to)
+
+    def origin(e):
+        if e == 0:
+            return None, zl
+        if e < 4:
+            return zl >= e, zl - e
+        return zl + (e - 3) < 4, zl + (e - 3)
+
+    def guarded(e, body):
+        here, bz = origin(e)
+        if here is None:
+            body(bz)
+        else:
+            pl.when(here)(lambda: body(bz))
+
+    def w_from_z(e):
+        def body(bz):
+            block = x * 4 + bz
+            for c in range(WCH):
+                wait_bytes(w_piece(block, c), wz_r.at[e - 1, c])
+                if e not in (3, 6):
+                    w_to_z(block, e < 4, e if e < 4 else e - 3, c)
+                w_to_x(block, e, c)
+                w_sibling(block, c)
+
+        guarded(e, body)
+
+    def w_from_x(e, pieces):
+        def body(bz):
+            for kx, c in pieces:
+                block = xb[kx] * 4 + bz
+                piece = w_piece(block, c)
+                wait_bytes(piece, wx_r.at[kx - 1, e, c])
+                if (kx, c) in PASSED:
+                    send(piece, piece, big_s.at[1], wx_r.at[1, e, c], x_peers[kx])
+                w_sibling(block, c)
+
+        guarded(e, body)
 
     def spread(buf, me, peers, n):
         slot = buf.at[me]
@@ -313,29 +350,16 @@
     for n in range(3):
         local[n].wait()
     for c in range(WCH):
+        w_to_z(pas, True, 0, c)
+        w_to_z(pas, False, 0, c)
         w_to_x(pas, 0, c)
-    w_to_z(1)
-    a_to_z(0)
-    for c in range(ACH):
-        a_to_y(0, tp, c)
-
-    w_from_x(0, PASSED)
-    w_from_z(1)
-    w_to_z(3)
-
-    collect(r1a, 16, 0)
-    r1b[tp] = jnp.sum(r1a[...], axis=0)
-    spread(r1b, tp, tp_peers, 1)
-
-    a_from_y(0, 0)
-    a_from_y(0, 1)
-    a_from_z(0)
-    a_to_z(1)
-    w_from_x(1, PASSED)
-    w_from_x(0, KEPT)
-
-    collect(r1b, 8, 1)
-    state0 = unpack8(jnp.sum(r1b[...], axis=0))
+
+    st = {}
+
+    def c1():
+        collect(r1a, 16, 0)
+        r1b[tp] = jnp.sum(r1a[...], axis=0)
+        spread(r1b, tp, tp_peers, 1)
 
     def scaled(state, g):
         ss = jnp.sum(state * state, axis=1, keepdims=True)
@@ -344,83 +368,110 @@
     def rms(ss):
         return lax.rsqrt(ss * (1.0 / D) + 1e-06)
 
-    a, ss = scaled(state0, g_self)
-    parts = []
-    for n, w in ((4, sq_v), (5, sk_v), (6, sv_v)):
-        local[n].wait()
-        parts.append(pack8(jnp.dot(a, w[...], preferred_element_type=F32)[:4]))
-    parts.append(jnp.broadcast_to(pad8(ss), (8, 128)))
-    merge_pas(jnp.concatenate(parts, axis=1), r2, r2z, 2)
-
-    a_from_y(0, 2)
-    a_from_y(0, 3)
-    w_from_z(3)
-    w_to_z(2)
-    merge_pas_z(r2, r2z, 2)
-
-    a_from_y(1, 0)
-    a_from_z(1)
-    a_to_z(2)
-    w_from_x(3, PASSED)
-    w_from_x(1, KEPT)
-
-    total = merged(r2z, 2)
-    scale = rms(total[:4, 768:769])
-    q, k, v = [unpack8(total[:, 256 * n : 256 * n + 256]) * scale for n in range(3)]
-    none = jnp.zeros((124, COLS), F32)
-    keys = jnp.concatenate([k, none], axis=0).astype(BF)
-    values = jnp.concatenate([v, none], axis=0).astype(BF)
-    step = lax.broadcasted_iota(jnp.int32, (32, 128), 0)
-    other = lax.broadcasted_iota(jnp.int32, (32, 128), 1)
-    _, weight, accum = attend(q.astype(BF).astype(F32), keys, values, other * 8 <= step)
-    heads = own_head(accum / weight)
-    local[7].wait()
-    r3[tp] = pack8(jnp.dot(pad8(heads).astype(BF), so_v[...], preferred_element_type=F32)[:4])
-    spread(r3, tp, tp_peers, 3)
-
-    a_from_y(1, 1)
-    w_from_z(2)
-    a_from_z(2)
-    a_to_z(3)
-
-    collect(r3, 8, 3)
-    state1 = state0 + unpack8(jnp.sum(r3[...], axis=0))
-    a, ss = scaled(state1, g_cross)
-    local[8].wait()
-    part = jnp.dot(a, cq_v[...], preferred_element_type=F32)[:4]
-    part = jnp.concatenate([pack8(part), jnp.broadcast_to(pad8(ss), (8, 128))], axis=1)
-    merge_pas(part, r4, r4z, 4)
-
-    w_from_x(2, PASSED)
-    w_from_x(3, KEPT)
-    a_from_y(1, 2)
-    merge_pas_z(r4, r4z, 4)
-    a_from_z(3)
-    w_from_x(2, KEPT)
-    a_from_y(1, 3)
-
-    for half in range(2):
-        wait_bytes(a_all.at[:, pl.ds(0, 2 * COLS)], an_r.at[half])
-    wait_bytes(w_all.at[0, pl.ds(0, 15 * OWN)], ws_r.at[0])
-    for c in range(2):
-
-        def tile(n, carry):
-            cols = pl.ds(pl.multiple_of(n * 256, 256), 256)
-            kv[c, :, cols] = jnp.dot(
-                a_all[...], w_all[c, :, cols], preferred_element_type=F32
-            ).astype(BF)
-            return carry
-
-        lax.fori_loop(0, 2, tile, 0)
+    def c2():
+        collect(r1b, 8, 1)
+        st["state0"] = unpack8(jnp.sum(r1b[...], axis=0))
+        a, ss = scaled(st["state0"], g_self)
+        parts = []
+        for n, w in ((4, sq_v), (5, sk_v), (6, sv_v)):
+            local[n].wait()
+            parts.append(pack8(jnp.dot(a, w[...], preferred_element_type=F32)[:4]))
+        parts.append(jnp.broadcast_to(pad8(ss), (8, 128)))
+        merge_pas(jnp.concatenate(parts, axis=1), r2, r2z, 2)
+
+    def c2z():
+        merge_pas_z(r2, r2z, 2)
+
+    def c3():
+        total = merged(r2z, 2)
+        scale = rms(total[:4, 768:769])
+        q, k, v = [unpack8(total[:, 256 * n : 256 * n + 256]) * scale for n in range(3)]
+        none = jnp.zeros((124, COLS), F32)
+        keys = jnp.concatenate([k, none], axis=0).astype(BF)
+        values = jnp.concatenate([v, none], axis=0).astype(BF)
+        step = lax.broadcasted_iota(jnp.int32, (32, 128), 0)
+        other = lax.broadcasted_iota(jnp.int32, (32, 128), 1)
+        _, weight, accum = attend(q.astype(BF).astype(F32), keys, values, other * 8 <= step)
+        heads = own_head(accum / weight)
+        local[7].wait()
+        r3[tp] = pack8(jnp.dot(pad8(heads).astype(BF), so_v[...], preferred_element_type=F32)[:4])
+        spread(r3, tp, tp_peers, 3)
+
+    def c4():
+        collect(r3, 8, 3)
+        st["state1"] = st["state0"] + unpack8(jnp.sum(r3[...], axis=0))
+        a, ss = scaled(st["state1"], g_cross)
+        local[8].wait()
+        part = jnp.dot(a, cq_v[...], preferred_element_type=F32)[:4]
+        part = jnp.concatenate([pack8(part), jnp.broadcast_to(pad8(ss), (8, 128))], axis=1)
+        merge_pas(part, r4, r4z, 4)
+
+    def c4z():
+        merge_pas_z(r4, r4z, 4)
+
+    def c5():
+        total = merged(r4z, 4)
+        st["cquery"] = unpack8(total[:, :256]) * rms(total[:4, 256:257])
+
+    near = pl.ds(pl.multiple_of(zh * HALF, HALF), HALF)
+    distant = pl.ds(pl.multiple_of((1 - zh) * HALF, HALF), HALF)
+
+    def a_whole(half, c):
+        wait_bytes(a_all.at[pl.ds(0, ARO), pl.ds(0, 2 * COLS)], an_r.at[half, c])
+
+    def mm(part=None):
+        if part is None:
+            for c in range(ACH):
+                a_whole(0, c)
+            wait_bytes(w_all.at[0, pl.ds(0, 15 * OWN)], ws_r.at[0])
+            rows, n_rows, cols = pl.ds(0, ROWS), ROWS, near
+        else:
+            for c in (2 * part, 2 * part + 1):
+                a_whole(1, c)
+            rows, n_rows, cols = pl.ds(part * 256, 256), 256, distant
+        for c in range(2):
+
+            def tile(n, carry):
+                to = pl.ds(pl.multiple_of(n * 256, 256), 256)
+                new = jnp.dot(a_all[rows, cols], w_all[c, cols, to], preferred_element_type=F32)
+                if part is None:
+                    sums[c, rows, to] = new
+                else:
+                    kv[c, rows, to] = (sums[c, rows, to] + new).astype(BF)
+                return carry
+
+            lax.fori_loop(0, 2, tile, 0)
+
+    def sy():
+        for c in range(ACH):
+            a_to_y(0, tp, c)
+
+    events = {
+        "sz": a_to_z,
+        "sy": sy,
+        "az": a_from_z,
+        "ay": a_from_y,
+        "wz": w_from_z,
+        "wp": lambda e: w_from_x(e, PASSED),
+        "wk": lambda e: w_from_x(e, KEPT),
+        "c1": c1,
+        "c2": c2,
+        "c2z": c2z,
+        "c3": c3,
+        "c4": c4,
+        "c4z": c4z,
+        "c5": c5,
+        "mm": mm,
+    }
+    for event in SCHEDULE:
+        events[event[0]](*event[1:])
+    state1, cquery = st["state1"], st["cquery"]
     outs = [
         pltpu.make_async_copy(kv.at[0], kout, osem.at[0]),
         pltpu.make_async_copy(kv.at[1], vout, osem.at[1]),
     ]
     for c in outs:
         c.start()
-
-    total = merged(r4z, 4)
-    cquery = unpack8(total[:, :256]) * rms(total[:4, 256:257])
 
     slot = lax.broadcasted_iota(jnp.int32, (32, ROWS), 1)
     live = (slot < lens[0]) | ((slot >= PLEN) & (slot < lens[1] + PLEN))
@@ -511,7 +562,13 @@
     ):
         wait_bytes(buf.at[pl.ds(0, count - 1)], es.at[n])
     wait_bytes(a_all.at[:, pl.ds(0, 7 * COLS)], big_s.at[0])
-    wait_bytes(w_all.at[0, pl.ds(0, 15 * OWN)], big_s.at[1])
+    wait_bytes(w_all.at[0, pl.ds(0, 12 * OWN)], big_s.at[1])
+    wait_bytes(w_all.at[0, pl.ds(0, OWN)], big_s.at[3])
+
+    @pl.when((zl > 0) & (zl < 3))
+    def _():
+        wait_bytes(w_all.at[0, pl.ds(0, 4 * OWN)], big_s.at[3])
+
     wait_bytes(w_all.at[0, pl.ds(0, 15 * OWN)], big_s.at[2])
     for c in outs:
         c.wait()
@@ -561,6 +618,7 @@
             pltpu.VMEM((ROWS, D), BF),
             pltpu.VMEM((2, D, COLS), BF),
             pltpu.VMEM((2, ROWS, COLS), BF),
+            pltpu.VMEM((2, ROWS, COLS), F32),
             pltpu.VMEM((VROWS, D), BF),
             pltpu.VMEM((OWN, COLS), BF),
             pltpu.VMEM((OWN, COLS), BF),
@@ -587,11 +645,11 @@
             dma((2,)),
             dma((ACH,)),
             dma((2, ACH)),
-            dma((2,)),
-            dma((3, WCH)),
-            dma((3, 4, WCH)),
+            dma((2, ACH)),
+            dma((6, WCH)),
+            dma((3, 7, WCH)),
             dma((1,)),
-            dma((3,)),
+            dma((4,)),
             dma((12,)),
             dma((12,)),
         ],

time: 115 us -> 107 us (0.930)
  Pallas kernels: 114 us -> 107 us
    pallas_call x1, Pallas kernels: 112 us -> 104 us  [shards(): pl.pallas_call(kernel, name='decoder_layer', out_shape=(jax.ShapeDtypeStr...]
where the time goes in v3:
time: 107 us
  Pallas kernels  107 us (100%)
    pallas_call x1, Pallas kernels, shards(): pl.pallas_call(kernel, name='decoder_layer', out_shape=(jax.ShapeDtypeStr...  104 us
    pallas_call x1, Pallas kernels, shards(): pl.pallas_call(finish, name='finish', out_shape=tuple((jax.ShapeDtypeStru...  2.21 us

profile of v3, /device:TPU:6, one launch (start us, length us, event | category | flops | bytes accessed | tf_op | source)
XLA Modules:
  0.0 107.2 jit_solution(10259724902970977866)
XLA Ops:
  0.6 104.4 %decoder_layer.1 = (f32[4,32]{1,0:T(4,128)}, bf16[512,512]{1,0:T(8,128)(2,1)}, bf16[512,512]{1,0:T(8,128)(2,1)}) custom-call(s32[4]{0:T(128)} %tok.1, s32[2]{0:T(128)} %lens.1, f32[32,128]{1,0:T(8,128)} %bitcast.3, f32[32,128]{1,0:T(8,128)} %bitcast.4, f32[32,128]{1,0:T(8,128)} %bitcast.5, bf16[512,512]{1,0:T(8,128)(2,1)} %passages.1, ...), custom_call_target="tpu_custom_call" | custom-call | flops 4294967296 | bytes 16777216 | tf_op jit(solution)/shard_map/decoder_layer/pallas_call | solution.py:607
  105.0 2.2 %finish.1 = (f32[4,32]{1,0:T(4,128)}, bf16[512,512]{1,0:T(8,128)(2,1)}, bf16[512,512]{1,0:T(8,128)(2,1)}) custom-call(f32[4,32]{1,0:T(4,128)} %get-tuple-element.6.out_a, bf16[512,512]{1,0:T(8,128)(2,1)} %get-tuple-element.7.k_a, bf16[512,512]{1,0:T(8,128)(2,1)} %get-tuple-element.8.v_a), custom_call_target="tpu_custom_call" | custom-call | tf_op jit(solution)/shard_map/finish/pallas_call | solution.py:682

commit v4 on v3

--- a/solution.py
+++ b/solution.py
@@ -17,22 +17,22 @@
 OWN = 256
 FFC = 1280
 VROWS = 251
-ACH = 4
+AROW = (0, 128, 256, 384, 512)
+ACH = len(AROW) - 1
+STRAIGHT = ((1, 3),)
 WCH = 2
-ARO = ROWS // ACH
 WRO = OWN // WCH
-PASSED = ((1, 0), (3, 1))
-KEPT = ((1, 1), (3, 0), (2, 0), (2, 1))
+PASSED = tuple((1 if c % 2 == 0 else 3, c) for c in range(WCH))
+KEPT = tuple((3 if c % 2 == 0 else 1, c) for c in range(WCH)) + tuple((2, c) for c in range(WCH))
 HALF = D // 2
 
 SCHEDULE = (
-    ("sz", 0), ("sy",), ("wp", 0), ("sz", 1), ("wz", 1), ("wz", 4), ("c1",),
-    ("ay", 0, 0), ("ay", 0, 1), ("az", 0), ("sz", 2), ("wp", 1), ("wp", 4), ("wk", 0), ("c2",),
-    ("ay", 0, 2), ("ay", 0, 3), ("wz", 2), ("wz", 5), ("c2z",),
-    ("ay", 1, 0), ("az", 1), ("sz", 3), ("wp", 2), ("wp", 5), ("wk", 1), ("wk", 4), ("c3",),
-    ("ay", 1, 1), ("wz", 3), ("wz", 6), ("az", 2), ("c4",),
-    ("wp", 3), ("wp", 6), ("wk", 2), ("wk", 5), ("ay", 1, 2), ("c4z",),
-    ("az", 3), ("wk", 3), ("wk", 6), ("ay", 1, 3), ("mm",), ("mm", 0), ("mm", 1), ("c5",),
+    ("sw",), ("sz", 0), ("sy",), ("wp", 0), ("wz", 1), ("wz", 4), ("sz", 1), ("ay", 0, 0), ("ay", 0, 1),
+    ("c1",), ("wp", 1), ("wp", 4), ("wz", 2), ("wz", 5), ("az", 0), ("sz", 2), ("ay", 0, 2), ("ay", 0, 3),
+    ("wk", 0), ("wp", 2), ("wp", 5), ("c2",), ("wz", 3), ("c2z",), ("wz", 6), ("az", 1), ("sz", 3),
+    ("ay", 1, 0), ("wp", 6), ("wk", 1), ("wk", 4), ("ay", 1, 1), ("wp", 3), ("c3",), ("az", 2), ("wk", 2),
+    ("wk", 5), ("ay", 1, 2), ("c4",), ("az", 3), ("wk", 3), ("wk", 6), ("c4z",), ("mm",), ("ay", 1, 3),
+    ("mm", 0), ("c5",), ("mm", 1),
 )
 
 
@@ -224,7 +224,7 @@
 
     def a_piece(block, c):
         cols = pl.ds(pl.multiple_of(block * COLS, COLS), COLS)
-        return a_all.at[pl.ds(c * ARO, ARO), cols]
+        return a_all.at[pl.ds(AROW[c], AROW[c + 1] - AROW[c]), cols]
 
     def w_piece(block, c):
         return w_all.at[pb, pl.ds(pl.multiple_of(block * OWN + c * WRO, WRO), WRO)]
@@ -236,8 +236,11 @@
     def a_to_y(half, block, c):
         piece = a_piece(block, c)
         for k, passed_on in ((1, c % 2 == 0), (3, c % 2 == 1)):
+            passed_on = passed_on and (half, c) not in STRAIGHT
             rsem = af_r.at[half, c] if passed_on else an_r.at[half, c]
             send(piece, piece, big_s.at[0], rsem, y_peers[k])
+        if (half, c) in STRAIGHT:
+            send(piece, piece, big_s.at[0], an_r.at[half, c], y_peers[2])
 
     def a_from_z(c):
         block = (1 - zh) * 4 + y
@@ -245,6 +248,8 @@
         a_to_y(1, block, c)
 
     def a_from_y(half, c):
+        if (half, c) in STRAIGHT:
+            return
         k = 1 if c % 2 == 0 else 3
         block = (zh if half == 0 else 1 - zh) * 4 + yb[k]
         piece = a_piece(block, c)
@@ -349,11 +354,6 @@
 
     for n in range(3):
         local[n].wait()
-    for c in range(WCH):
-        w_to_z(pas, True, 0, c)
-        w_to_z(pas, False, 0, c)
-        w_to_x(pas, 0, c)
-
     st = {}
 
     def c1():
@@ -417,18 +417,21 @@
     distant = pl.ds(pl.multiple_of((1 - zh) * HALF, HALF), HALF)
 
     def a_whole(half, c):
-        wait_bytes(a_all.at[pl.ds(0, ARO), pl.ds(0, 2 * COLS)], an_r.at[half, c])
+        blocks = 3 if (half, c) in STRAIGHT else 2
+        n = AROW[c + 1] - AROW[c]
+        wait_bytes(a_all.at[pl.ds(0, n), pl.ds(0, blocks * COLS)], an_r.at[half, c])
 
     def mm(part=None):
         if part is None:
             for c in range(ACH):
                 a_whole(0, c)
             wait_bytes(w_all.at[0, pl.ds(0, 15 * OWN)], ws_r.at[0])
-            rows, n_rows, cols = pl.ds(0, ROWS), ROWS, near
+            rows, cols = pl.ds(0, ROWS), near
         else:
             for c in (2 * part, 2 * part + 1):
                 a_whole(1, c)
-            rows, n_rows, cols = pl.ds(part * 256, 256), 256, distant
+            first, last = AROW[2 * part], AROW[2 * part + 2]
+            rows, cols = pl.ds(first, last - first), distant
         for c in range(2):
 
             def tile(n, carry):
@@ -442,12 +445,19 @@
 
             lax.fori_loop(0, 2, tile, 0)
 
+    def sw():
+        for c in range(WCH):
+            w_to_z(pas, True, 0, c)
+            w_to_z(pas, False, 0, c)
+            w_to_x(pas, 0, c)
+
     def sy():
         for c in range(ACH):
             a_to_y(0, tp, c)
 
     events = {
         "sz": a_to_z,
+        "sw": sw,
         "sy": sy,
         "az": a_from_z,
         "ay": a_from_y,

time: 107 us -> 106 us (level)
  Pallas kernels: 107 us -> 105 us
    pallas_call x1, Pallas kernels: 104 us -> 103 us  [shards(): pl.pallas_call(kernel, name='decoder_layer', out_shape=(jax.ShapeDtypeStr...]
where the time goes in v4:
time: 106 us
  Pallas kernels  105 us (99%)
    pallas_call x1, Pallas kernels, shards(): pl.pallas_call(kernel, name='decoder_layer', out_shape=(jax.ShapeDtypeStr...  103 us
    pallas_call x1, Pallas kernels, shards(): pl.pallas_call(finish, name='finish', out_shape=tuple((jax.ShapeDtypeStru...  2.21 us

profile of v4, /device:TPU:6, one launch (start us, length us, event | category | flops | bytes accessed | tf_op | source)
XLA Modules:
  0.0 105.7 jit_solution(2603466850739919353)
XLA Ops:
  0.6 102.8 %decoder_layer.1 = (f32[4,32]{1,0:T(4,128)}, bf16[512,512]{1,0:T(8,128)(2,1)}, bf16[512,512]{1,0:T(8,128)(2,1)}) custom-call(s32[4]{0:T(128)} %tok.1, s32[2]{0:T(128)} %lens.1, f32[32,128]{1,0:T(8,128)} %bitcast.3, f32[32,128]{1,0:T(8,128)} %bitcast.4, f32[32,128]{1,0:T(8,128)} %bitcast.5, bf16[512,512]{1,0:T(8,128)(2,1)} %passages.1, ...), custom_call_target="tpu_custom_call" | custom-call | flops 4294967296 | bytes 16777216 | tf_op jit(solution)/shard_map/decoder_layer/pallas_call | solution.py:617
  103.5 2.2 %finish.1 = (f32[4,32]{1,0:T(4,128)}, bf16[512,512]{1,0:T(8,128)(2,1)}, bf16[512,512]{1,0:T(8,128)(2,1)}) custom-call(f32[4,32]{1,0:T(4,128)} %get-tuple-element.6.out_a, bf16[512,512]{1,0:T(8,128)(2,1)} %get-tuple-element.7.k_a, bf16[512,512]{1,0:T(8,128)(2,1)} %get-tuple-element.8.v_a), custom_call_target="tpu_custom_call" | custom-call | tf_op jit(solution)/shard_map/finish/pallas_call | solution.py:692

commit v5 on v4

--- a/solution.py
+++ b/solution.py
@@ -19,7 +19,7 @@
 VROWS = 251
 AROW = (0, 128, 256, 384, 512)
 ACH = len(AROW) - 1
-STRAIGHT = ((1, 3),)
+STRAIGHT = ((1, 0), (1, 1), (1, 2), (1, 3))
 WCH = 2
 WRO = OWN // WCH
 PASSED = tuple((1 if c % 2 == 0 else 3, c) for c in range(WCH))
@@ -27,12 +27,12 @@
 HALF = D // 2
 
 SCHEDULE = (
-    ("sw",), ("sz", 0), ("sy",), ("wp", 0), ("wz", 1), ("wz", 4), ("sz", 1), ("ay", 0, 0), ("ay", 0, 1),
-    ("c1",), ("wp", 1), ("wp", 4), ("wz", 2), ("wz", 5), ("az", 0), ("sz", 2), ("ay", 0, 2), ("ay", 0, 3),
-    ("wk", 0), ("wp", 2), ("wp", 5), ("c2",), ("wz", 3), ("c2z",), ("wz", 6), ("az", 1), ("sz", 3),
-    ("ay", 1, 0), ("wp", 6), ("wk", 1), ("wk", 4), ("ay", 1, 1), ("wp", 3), ("c3",), ("az", 2), ("wk", 2),
-    ("wk", 5), ("ay", 1, 2), ("c4",), ("az", 3), ("wk", 3), ("wk", 6), ("c4z",), ("mm",), ("ay", 1, 3),
-    ("mm", 0), ("c5",), ("mm", 1),
+    ("sw",), ("sz", 0), ("sy", 0), ("sy", 1), ("sy", 2), ("sy", 3), ("e1",), ("wp", 0), ("wz", 1), ("wz", 4),
+    ("sz", 1), ("ay", 0, 0), ("ay", 0, 1), ("c1",), ("wp", 1), ("wp", 4), ("wz", 2), ("wz", 5), ("az", 0),
+    ("sz", 2), ("ay", 0, 2), ("ay", 0, 3), ("wk", 0), ("c2",), ("wp", 2), ("wp", 5), ("c2z",), ("wz", 3),
+    ("wz", 6), ("az", 1), ("sz", 3), ("ay", 1, 0), ("wp", 6), ("wk", 1), ("wk", 4), ("ay", 1, 1), ("wp", 3),
+    ("c3",), ("az", 2), ("wk", 2), ("wk", 5), ("ay", 1, 2), ("c4",), ("az", 3), ("wk", 3), ("wk", 6),
+    ("c4z",), ("mm",), ("ay", 1, 3), ("mm", 0), ("c5",), ("mm", 1),
 )
 
 
@@ -183,6 +183,11 @@
     z4_peer = (pb, pas, (1 - zh) * 4 + y)
     sibling = (1 - pb, pas, tp)
 
+    barrier = pltpu.get_barrier_semaphore()
+    greet = pas_peers + tp_peers + [sibling]
+    for d in greet:
+        pl.semaphore_signal(barrier, inc=1, device_id=d, device_id_type=MESH)
+
     pas0 = pl.multiple_of(pas * OWN, OWN)
     tp0 = pl.multiple_of(tp * COLS, COLS)
     loads = [
@@ -201,13 +206,8 @@
         (w_down, down_v),
     ]
     local = [pltpu.make_async_copy(s, d, lsem.at[n]) for n, (s, d) in enumerate(loads)]
-    for c in local:
+    for c in local[:3]:
         c.start()
-
-    barrier = pltpu.get_barrier_semaphore()
-    greet = pas_peers + tp_peers + [sibling]
-    for d in greet:
-        pl.semaphore_signal(barrier, inc=1, device_id=d, device_id_type=MESH)
 
     def send(src, dst, ssem, rsem, dev):
         pltpu.make_async_remote_copy(
@@ -337,24 +337,27 @@
     def gain(g):
         return jnp.concatenate([g[pl.ds(2 * pas, 1), :], g[pl.ds(2 * pas + 1, 1), :]], axis=1)
 
-    local[3].wait()
-    row = lax.broadcasted_iota(jnp.int32, (8, VROWS), 0)
-    place = lax.broadcasted_iota(jnp.int32, (8, VROWS), 1) + (pas * 8 + tp) * VROWS
-    wanted = jnp.full((8, VROWS), -1, jnp.int32)
-    for s in range(STEPS):
-        wanted = jnp.where(row == s, tok[s], wanted)
-    onehot = jnp.where(place == wanted, 1.0, 0.0).astype(BF)
-    mine = jnp.dot(onehot, emb_v[...], preferred_element_type=F32)
-    for i in range(16):
-        s1a[i] = pack8(mine[:4, OWN * i : OWN * i + OWN])
-    r1a[pas] = s1a[pas]
     pl.semaphore_wait(barrier, len(greet))
-    for p in pas_peers:
-        send(s1a.at[p[1]], r1a.at[pas], es.at[0], er.at[0], p)
-
     for n in range(3):
         local[n].wait()
+    for c in local[3:]:
+        c.start()
     st = {}
+
+    def e1():
+        local[3].wait()
+        row = lax.broadcasted_iota(jnp.int32, (8, VROWS), 0)
+        place = lax.broadcasted_iota(jnp.int32, (8, VROWS), 1) + (pas * 8 + tp) * VROWS
+        wanted = jnp.full((8, VROWS), -1, jnp.int32)
+        for s in range(STEPS):
+            wanted = jnp.where(row == s, tok[s], wanted)
+        onehot = jnp.where(place == wanted, 1.0, 0.0).astype(BF)
+        mine = jnp.dot(onehot, emb_v[...], preferred_element_type=F32)
+        for i in range(16):
+            s1a[i] = pack8(mine[:4, OWN * i : OWN * i + OWN])
+        r1a[pas] = s1a[pas]
+        for p in pas_peers:
+            send(s1a.at[p[1]], r1a.at[pas], es.at[0], er.at[0], p)
 
     def c1():
         collect(r1a, 16, 0)
@@ -451,9 +454,8 @@
             w_to_z(pas, False, 0, c)
             w_to_x(pas, 0, c)
 
-    def sy():
-        for c in range(ACH):
-            a_to_y(0, tp, c)
+    def sy(c):
+        a_to_y(0, tp, c)
 
     events = {
         "sz": a_to_z,
@@ -464,6 +466,7 @@
         "wz": w_from_z,
         "wp": lambda e: w_from_x(e, PASSED),
         "wk": lambda e: w_from_x(e, KEPT),
+        "e1": e1,
         "c1": c1,
         "c2": c2,
         "c2z": c2z,

time: 106 us -> 102 us (0.962)
  Pallas kernels: 105 us -> 102 us
    pallas_call x1, Pallas kernels: 103 us -> 99.3 us  [shards(): pl.pallas_call(kernel, name='decoder_layer', out_shape=(jax.ShapeDtypeStr...]
where the time goes in v5:
time: 102 us
  Pallas kernels  102 us (100%)
    pallas_call x1, Pallas kernels, shards(): pl.pallas_call(kernel, name='decoder_layer', out_shape=(jax.ShapeDtypeStr...  99.3 us
    pallas_call x1, Pallas kernels, shards(): pl.pallas_call(finish, name='finish', out_shape=tuple((jax.ShapeDtypeStru...  2.21 us

profile of v5, /device:TPU:6, one launch (start us, length us, event | category | flops | bytes accessed | tf_op | source)
XLA Modules:
  0.0 102.2 jit_solution(17362558440235312478)
XLA Ops:
  0.6 99.3 %decoder_layer.1 = (f32[4,32]{1,0:T(4,128)}, bf16[512,512]{1,0:T(8,128)(2,1)}, bf16[512,512]{1,0:T(8,128)(2,1)}) custom-call(s32[4]{0:T(128)} %tok.1, s32[2]{0:T(128)} %lens.1, f32[32,128]{1,0:T(8,128)} %bitcast.3, f32[32,128]{1,0:T(8,128)} %bitcast.4, f32[32,128]{1,0:T(8,128)} %bitcast.5, bf16[512,512]{1,0:T(8,128)(2,1)} %passages.1, ...), custom_call_target="tpu_custom_call" | custom-call | flops 4294967296 | bytes 16777216 | tf_op jit(solution)/shard_map/decoder_layer/pallas_call | solution.py:620
  100.0 2.2 %finish.1 = (f32[4,32]{1,0:T(4,128)}, bf16[512,512]{1,0:T(8,128)(2,1)}, bf16[512,512]{1,0:T(8,128)(2,1)}) custom-call(f32[4,32]{1,0:T(4,128)} %get-tuple-element.6.out_a, bf16[512,512]{1,0:T(8,128)(2,1)} %get-tuple-element.7.k_a, bf16[512,512]{1,0:T(8,128)(2,1)} %get-tuple-element.8.v_a), custom_call_target="tpu_custom_call" | custom-call | tf_op jit(solution)/shard_map/finish/pallas_call | solution.py:695

commit v6 on v5

--- a/solution.py
+++ b/solution.py
@@ -87,6 +87,17 @@
     total = jnp.sum(weights.astype(F32), axis=1, keepdims=True)
     accum = jnp.dot(weights, values, preferred_element_type=F32)
     return peak, total, accum
+
+
+def halve(total):
+    parts = [
+        jnp.concatenate([total[:, 256 * n : 256 * n + 128], total[:, 256 * n + 128 : 256 * n + 256]], axis=0)
+        for n in range(3)
+    ]
+    ss = total[:, 768:896]
+    hi = ss.astype(BF).astype(F32)
+    parts.append(jnp.concatenate([hi, ss - hi], axis=0))
+    return jnp.concatenate(parts, axis=1).astype(BF)
 
 
 def split_sum(ss):
@@ -326,7 +337,8 @@
 
     def merge_pas_z(bx, bz, n):
         wait_bytes(bx.at[pl.ds(0, 3)], er.at[n])
-        bz[zl] = bx[0] + bx[1] + bx[2] + bx[3]
+        total = bx[0] + bx[1] + bx[2] + bx[3]
+        bz[zl] = total if bz.dtype == F32 else halve(total)
         for k in (3, 2, 1):
             send(bz.at[zl], bz.at[zl], es.at[n + 7], er.at[n + 7], z_peers[k])
 
@@ -386,9 +398,16 @@
         merge_pas_z(r2, r2z, 2)
 
     def c3():
-        total = merged(r2z, 2)
-        scale = rms(total[:4, 768:769])
-        q, k, v = [unpack8(total[:, 256 * n : 256 * n + 256]) * scale for n in range(3)]
+        wait_bytes(r2z.at[pl.ds(0, 3)], er.at[9])
+        total = r2z[0].astype(F32)
+        for i in range(1, 4):
+            total = total + r2z[i].astype(F32)
+        scale = rms(total[:4, 384:385] + total[8:12, 384:385])
+        whole = [
+            jnp.concatenate([total[:8, 128 * n : 128 * n + 128], total[8:, 128 * n : 128 * n + 128]], axis=1)
+            for n in range(3)
+        ]
+        q, k, v = [unpack8(w) * scale for w in whole]
         none = jnp.zeros((124, COLS), F32)
         keys = jnp.concatenate([k, none], axis=0).astype(BF)
         values = jnp.concatenate([v, none], axis=0).astype(BF)
@@ -646,7 +665,7 @@
             pltpu.VMEM((16, 8, 128), F32),
             pltpu.VMEM((8, 8, 128), F32),
             pltpu.VMEM((4, 8, 896), F32),
-            pltpu.VMEM((4, 8, 896), F32),
+            pltpu.VMEM((4, 16, 512), BF),
             pltpu.VMEM((8, 8, 128), F32),
             pltpu.VMEM((4, 8, 384), F32),
             pltpu.VMEM((4, 8, 384), F32),

time: 102 us -> 103 us (level); the launches traced: 102 us -> 102 us
  no operation moved by 1% of the time
where the time goes in v6:
time: 103 us; the launch traced here: 102 us
  Pallas kernels  101 us (98%)
    pallas_call x1, Pallas kernels, shards(): pl.pallas_call(kernel, name='decoder_layer', out_shape=(jax.ShapeDtypeStr...  99 us
    pallas_call x1, Pallas kernels, shards(): pl.pallas_call(finish, name='finish', out_shape=tuple((jax.ShapeDtypeStru...  2.21 us

profile of v6, /device:TPU:6, one launch (start us, length us, event | category | flops | bytes accessed | tf_op | source)
XLA Modules:
  0.0 101.9 jit_solution(17353303148680175277)
XLA Ops:
  0.6 99.0 %decoder_layer.1 = (f32[4,32]{1,0:T(4,128)}, bf16[512,512]{1,0:T(8,128)(2,1)}, bf16[512,512]{1,0:T(8,128)(2,1)}) custom-call(s32[4]{0:T(128)} %tok.1, s32[2]{0:T(128)} %lens.1, f32[32,128]{1,0:T(8,128)} %bitcast.3, f32[32,128]{1,0:T(8,128)} %bitcast.4, f32[32,128]{1,0:T(8,128)} %bitcast.5, bf16[512,512]{1,0:T(8,128)(2,1)} %passages.1, ...), custom_call_target="tpu_custom_call" | custom-call | flops 4294967296 | bytes 16777216 | tf_op jit(solution)/shard_map/decoder_layer/pallas_call | solution.py:639
  99.7 2.2 %finish.1 = (f32[4,32]{1,0:T(4,128)}, bf16[512,512]{1,0:T(8,128)(2,1)}, bf16[512,512]{1,0:T(8,128)(2,1)}) custom-call(f32[4,32]{1,0:T(4,128)} %get-tuple-element.6.out_a, bf16[512,512]{1,0:T(8,128)(2,1)} %get-tuple-element.7.k_a, bf16[512,512]{1,0:T(8,128)(2,1)} %get-tuple-element.8.v_a), custom_call_target="tpu_custom_call" | custom-call | tf_op jit(solution)/shard_map/finish/pallas_call | solution.py:714
